TPU v7x, 32 devices: a whole 2x2x4 slice. The times are simulated.
32 devices in a mesh: ctx: 8 (over y, x, core), head: 4 (over z).
Axes of the slice: x: 2, y: 2, z: 4, core: 2. Of those that a mesh axis runs over, the one named last changes fastest.
Arguments:
- queries: bfloat16 [1024, 4096], P('ctx', 'head'), may hold values from -6 to 6
- key_input: bfloat16 [2, 1024, 4096], P(None, 'ctx', 'head'), may hold values from -6 to 6
- value_input: bfloat16 [2, 1024, 4096], P(None, 'ctx', 'head'), may hold values from -6 to 6
- beta_rates: float32 [32, 2, 1024], P('head', None, 'ctx'), may hold values from 0 to 1.9, as said below
- out_grad: bfloat16 [1024, 4096], P(('ctx', 'head')), may hold values from -0.75 to 0.75
- out_weight: bfloat16 [4096, 4096], P('head'), may hold values from -0.09375 to 0.09375
Outputs:
- grad_queries: bfloat16 [1024, 4096], P('ctx', 'head')
- grad_keys: bfloat16 [2, 1024, 4096], P(None, 'ctx', 'head')
- grad_values: bfloat16 [2, 1024, 4096], P(None, 'ctx', 'head')
- grad_rates: float32 [32, 2, 1024], P('head', None, 'ctx')
Inputs may be any that keep to these rules, and one draw needn't show every extreme that they name: `beta_rates`: positive strengths.
All inputs are finite; a program needn't handle non-finite values.
Results may differ from a plain program's by a relative error of at most 0.011.
Values may be sent and summed in bfloat16 or wider, within the bound.
A program may use at most 192 MiB of HBM per device.

v0:
```python
import jax
import jax.numpy as jnp
from jax import lax
from jax.sharding import PartitionSpec as P

HEAD_DIM = 128
BLOCK = 64


highest = lax.Precision.HIGHEST


def shifted(value, axis, by):
    count = lax.axis_size(axis)
    pairs = [(i, i + by) for i in range(count) if 0 <= i + by < count]
    return lax.ppermute(value, axis, pairs)


def block_solve(key_rows, value_rows, rate_rows):
    length = key_rows.shape[1]
    gram = jnp.einsum("bik,bjk->bij", key_rows, key_rows, precision=highest)
    strict = jnp.tril(jnp.ones((length, length), key_rows.dtype), -1)
    system = jnp.eye(length, dtype=key_rows.dtype) + gram * rate_rows[:, None, :] * strict
    joined = jnp.concatenate([key_rows, value_rows], axis=2)
    solved = jax.scipy.linalg.solve_triangular(system, joined, lower=True, unit_diagonal=True)
    return (solved[..., : key_rows.shape[2]], solved[..., key_rows.shape[2] :])


def read_mask(query_rows, length, dtype):
    house_count = length // query_rows
    upper = house_count * (jnp.arange(query_rows) + 1)
    return (jnp.arange(length)[None, :] < upper[:, None]).astype(dtype)


def solved_step(state_in, pieces):
    query_rows, key_rows, rate_rows, solved_k, solved_v = pieces
    errors = jnp.einsum("bik,bkv->biv", solved_k, state_in, precision=highest) - solved_v
    weighted = errors * rate_rows[:, :, None]
    scores = jnp.einsum("btk,bik->bti", query_rows, key_rows, precision=highest)
    scores = scores * read_mask(query_rows.shape[1], key_rows.shape[1], scores.dtype)[None]
    outputs = jnp.einsum("btk,bkv->btv", query_rows, state_in, precision=highest)
    outputs = outputs - jnp.einsum("bti,biv->btv", scores, weighted, precision=highest)
    state_out = state_in - jnp.einsum("bik,biv->bkv", key_rows, weighted, precision=highest)
    return (state_out, outputs)


def arrange(query_all, raw_keys, value_all, rate_all, block_len):
    tokens, head_count, head_width = query_all.shape
    house_count = raw_keys.shape[0]
    scaling = lax.rsqrt(jnp.sum(raw_keys * raw_keys, axis=-1, keepdims=True) + 1e-06)
    normed = raw_keys * scaling
    blocks = tokens // block_len
    query_blocks = query_all.reshape(blocks, block_len, head_count, head_width).transpose(
        0, 2, 1, 3
    )

    def reorder(tensor):
        last_width = tensor.shape[-1]
        shaped = tensor.reshape(house_count, blocks, block_len, head_count, last_width)
        return shaped.transpose(1, 3, 2, 0, 4).reshape(
            blocks, head_count, block_len * house_count, last_width
        )

    rate_blocks = rate_all.reshape(head_count, house_count, blocks, block_len)
    rate_blocks = rate_blocks.transpose(2, 0, 3, 1).reshape(
        blocks, head_count, block_len * house_count
    )
    return (query_blocks, reorder(normed), reorder(value_all), rate_blocks)


def matmul_heads(left, right):
    return jnp.einsum("hij,hjk->hik", left, right, precision=highest)


def compose(earlier, later):
    return (matmul_heads(later[0], earlier[0]), matmul_heads(later[0], earlier[1]) + later[1])


def shards(queries, key_input, value_input, beta_rates, out_grad, out_weight):
    d_attn = lax.dot_general(
        lax.all_gather(out_grad, "head", axis=0, tiled=True),
        out_weight,
        (((1,), (1,)), ((), ())),
        preferred_element_type=jnp.float32,
    ).astype(jnp.bfloat16)
    tokens = queries.shape[0]
    head_count = queries.shape[1] // HEAD_DIM
    house_count = key_input.shape[0]
    query_all = queries.astype(jnp.float32).reshape(tokens, head_count, HEAD_DIM)
    raw_keys = key_input.astype(jnp.float32).reshape(house_count, tokens, head_count, HEAD_DIM)
    value_all = value_input.astype(jnp.float32).reshape(house_count, tokens, head_count, HEAD_DIM)
    grad_out = d_attn.astype(jnp.float32).reshape(tokens, head_count, HEAD_DIM)
    blocks = tokens // BLOCK
    rows_block = BLOCK * house_count

    def arrange_scaled(query_arg, key_arg, value_arg, rate_arg):
        return arrange(query_arg * HEAD_DIM ** (-0.5), key_arg, value_arg, rate_arg, BLOCK)

    arranged, arrange_pull = jax.vjp(arrange_scaled, query_all, raw_keys, value_all, beta_rates)
    query_blocks, key_blocks, value_blocks, rate_blocks = arranged
    flat_shape = (blocks * head_count, rows_block, HEAD_DIM)
    block_shape = (blocks, head_count, rows_block, HEAD_DIM)
    solved_flat, solve_pull = jax.vjp(
        block_solve,
        key_blocks.reshape(flat_shape),
        value_blocks.reshape(flat_shape),
        rate_blocks.reshape(blocks * head_count, rows_block),
    )
    solved_k = solved_flat[0].reshape(block_shape)
    solved_v = solved_flat[1].reshape(block_shape)
    grad_blocks = grad_out.reshape(blocks, BLOCK, head_count, HEAD_DIM).transpose(0, 2, 1, 3)
    identity_b = jnp.broadcast_to(
        jnp.eye(HEAD_DIM, dtype=jnp.float32), (head_count, HEAD_DIM, HEAD_DIM)
    )
    zero_b = jnp.zeros((head_count, HEAD_DIM, HEAD_DIM), jnp.float32)

    def block_maps(pieces):
        query_rows, key_rows, rate_rows, solved_kr, solved_vr, grad_rows = pieces
        scaled_keys = key_rows * rate_rows[:, :, None]
        transfer = identity_b - jnp.einsum(
            "bik,bil->bkl", scaled_keys, solved_kr, precision=highest
        )
        offset = jnp.einsum("bik,biv->bkv", scaled_keys, solved_vr, precision=highest)
        scores = jnp.einsum("btk,bik->bti", query_rows, key_rows, precision=highest)
        scores = (
            scores
            * read_mask(query_rows.shape[1], key_rows.shape[1], scores.dtype)[None]
            * rate_rows[:, None, :]
        )
        reading = query_rows - jnp.einsum("bti,bik->btk", scores, solved_kr, precision=highest)
        local_grad = jnp.einsum("btk,btv->bkv", reading, grad_rows, precision=highest)
        return (transfer, offset, local_grad)

    transfers, offsets, local_grads = lax.map(
        block_maps, (query_blocks, key_blocks, rate_blocks, solved_k, solved_v, grad_blocks)
    )

    def forward_fold(carried, pieces):
        return (compose(carried, pieces), None)

    (device_p, device_r), unused = lax.scan(
        forward_fold, (identity_b, zero_b), (transfers, offsets)
    )

    def adjoint_fold(carried, pieces):
        transfer, local_grad = pieces
        return (matmul_heads(jnp.swapaxes(transfer, 1, 2), carried) + local_grad, None)

    device_g, unused_two = lax.scan(adjoint_fold, zero_b, (transfers, local_grads), reverse=True)

    def forward_turn(counter, carried):
        return shifted(matmul_heads(device_p, carried) + device_r, "ctx", 1)

    start_state = lax.fori_loop(0, lax.axis_size("ctx") - 1, forward_turn, zero_b)
    transposed_p = jnp.swapaxes(device_p, 1, 2)

    def backward_turn(counter, carried):
        return shifted(matmul_heads(transposed_p, carried) + device_g, "ctx", -1)

    end_grad = lax.fori_loop(0, lax.axis_size("ctx") - 1, backward_turn, zero_b)

    def local_forward(query_arg, key_arg, rate_arg, solved_k_arg, solved_v_arg):
        final, outputs_all = lax.scan(
            solved_step, start_state, (query_arg, key_arg, rate_arg, solved_k_arg, solved_v_arg)
        )
        return (outputs_all, final)

    outputs_pair, pullback = jax.vjp(
        local_forward, query_blocks, key_blocks, rate_blocks, solved_k, solved_v
    )
    grad_qb, grad_kb, grad_rb, grad_sk, grad_sv = pullback((grad_blocks, end_grad))
    solve_k, solve_v, solve_r = solve_pull(
        (grad_sk.reshape(flat_shape), grad_sv.reshape(flat_shape))
    )
    grad_kb = grad_kb + solve_k.reshape(block_shape)
    grad_vb = solve_v.reshape(block_shape)
    grad_rb = grad_rb + solve_r.reshape(blocks, head_count, rows_block)
    grad_q, grad_k, grad_v, grad_b = arrange_pull((grad_qb, grad_kb, grad_vb, grad_rb))
    return (
        grad_q.reshape(tokens, head_count * HEAD_DIM).astype(jnp.bfloat16),
        grad_k.reshape(house_count, tokens, head_count * HEAD_DIM).astype(jnp.bfloat16),
        grad_v.reshape(house_count, tokens, head_count * HEAD_DIM).astype(jnp.bfloat16),
        grad_b,
    )


def solution(mesh):
    placed = (
        P("ctx", "head"),
        P(None, "ctx", "head"),
        P(None, "ctx", "head"),
        P("head", None, "ctx"),
        P(("ctx", "head"), None),
        P("head", None),
    )
    return jax.shard_map(
        shards,
        mesh=mesh,
        in_specs=placed,
        out_specs=(
            P("ctx", "head"),
            P(None, "ctx", "head"),
            P(None, "ctx", "head"),
            P("head", None, "ctx"),
        ),
        check_vma=False,
    )
```

profile of v0, /device:TPU:19, one launch (start us, length us, event | category | flops | bytes accessed | tf_op | source)
XLA Modules:
  0.0 530.1 jit_solution(8644275983539148851)
XLA Ops:
  11.6 2.3 fusion.144
  15.1 157.2 %custom-call.10 = f32[16,1,128,128]{2,3,1,0:T(8,128)S(1)} custom-call(f32[16,1,128,128]{3,2,1,0:T(8,128)S(1)} %add_bitcast_fusion), custom_call_target="InvertDiagBlocksLowerTriangular" | custom-call | tf_op jit(solution)/shard_map/jvp(jit(_solve_triangular))/vmap()/triangular_solve | solution.py:25
  177.4 2.4 mul.236
  179.8 3.2 fusion.117
  185.6 6.6 %fusion.126 = f32[16,8,8,128]{3,1,2,0:T(8,128)S(1)} fusion(bf16[128,4096]{1,0:T(8,128)(2,1)} %all-gather.2.cloned.1.call-done, bf16[1024,4096]{1,0:T(8,128)(2,1)} %param.25), kind=kOutput, calls=%fused_computation.167 | convolution fusion | flops 1074003968 | bytes 9961472 | tf_op jit(solution)/shard_map/dot_general | solution.py:80
  195.8 15.8 %while.111 = (s32[]{:T(128)}, f32[2,8,128,128]{3,2,1,0:T(8,128)}, f32[2,8,128,128]{3,2,1,0:T(8,128)}, f32[2,8,128,128]{3,2,1,0:T(8,128)}, f32[2,8,128,128]{3,2,1...) while((s32[]{:T(128)}, f32[2,8,128,128]{3,2,1,0:T(8,128)}, ...), condition=%wide.region_2.3_spmd.clone, body=%wide.region_1.2_spmd.clone.sunk | while | flops 705249408 | bytes 19294924 | solution.py:134
  212.6 12.6 %while.114 = (s32[]{:T(128)}, f32[8,128,128]{2,1,0:T(8,128)}, f32[8,128,128]{2,1,0:T(8,128)}, f32[2,8,128,128]{3,2,1,0:T(8,128)}, f32[2,8,128,128]{3,2,1,0:T(8,128)}, /*index=5*/s32[]{:T(128)}, s32[]{:T(128)}) while((s32[]{:T(128)}, f32[8,128,128]{2,1,0:T(8,128)}, f32[8,128,128]{2,1,0:T(8,128)}, f32[2,8,128,128]{3,2,1,0:T(8,128)}, ...), condition=%wide.region_4.5_spmd.clone, body=%wide.region_3.4_spmd.clone.sunk | while | flops 402915328 | bytes 7865971 | solution.py:141
  213.7 2.6 convolution_add_fusion.21
  216.4 2.5 fusion.266
  220.0 2.6 convolution_add_fusion.21
  222.7 2.5 fusion.266
  225.2 98.5 %while.110 = (s32[]{:T(128)}, f32[8,128,128]{2,1,0:T(8,128)S(1)}, f32[8,128,128]{2,1,0:T(8,128)}, f32[8,128,128]{2,1,0:T(8,128)}, s32[]{:T(128)}) while((s32[]{:T(128)}, f32[8,128,128]{2,1,0:T(8,128)S(1)}, f32[8,128,128]{2,1,0:T(8,128)}, f32[8,128,128]{2,1,0:T(8,128)}, s32[]{:T(128)}) %tuple.200), condition=%wide.region_10.11_spmd, body=%wide.region_9.10_spmd.sunk | while | flops 201457664 | bytes 4194405 | solution.py:154
  225.2 2.7 convolution_add_fusion.18
  227.9 3.7 collective-permute-start.1
  231.6 6.4 %collective-permute-done.1 = f32[8,128,128]{2,1,0:T(8,128)S(1)} collective-permute-done((f32[8,128,128]{2,1,0:T(8,128)}, f32[8,128,128]{2,1,0:T(8,128)S(1)}, u32[]{:S(2)}, u32[]{:S(2)}) %collective-permute-start.1) | collective-permute-done | bytes 524320 | tf_op jit(solution)/shard_map/while/body/eval_jaxpr/ppermute | solution.py:16
  238.0 2.7 convolution_add_fusion.18
  240.7 5.2 collective-permute-start.1
  245.9 6.4 %collective-permute-done.1 = f32[8,128,128]{2,1,0:T(8,128)S(1)} collective-permute-done((f32[8,128,128]{2,1,0:T(8,128)}, f32[8,128,128]{2,1,0:T(8,128)S(1)}, u32[]{:S(2)}, u32[]{:S(2)}) %collective-permute-start.1) | collective-permute-done | bytes 524320 | tf_op jit(solution)/shard_map/while/body/eval_jaxpr/ppermute | solution.py:16
  252.3 2.7 convolution_add_fusion.18
  255.0 5.2 collective-permute-start.1
  260.2 6.4 %collective-permute-done.1 = f32[8,128,128]{2,1,0:T(8,128)S(1)} collective-permute-done((f32[8,128,128]{2,1,0:T(8,128)}, f32[8,128,128]{2,1,0:T(8,128)S(1)}, u32[]{:S(2)}, u32[]{:S(2)}) %collective-permute-start.1) | collective-permute-done | bytes 524320 | tf_op jit(solution)/shard_map/while/body/eval_jaxpr/ppermute | solution.py:16
  266.6 2.7 convolution_add_fusion.18
  269.3 5.2 collective-permute-start.1
  274.5 6.4 %collective-permute-done.1 = f32[8,128,128]{2,1,0:T(8,128)S(1)} collective-permute-done((f32[8,128,128]{2,1,0:T(8,128)}, f32[8,128,128]{2,1,0:T(8,128)S(1)}, u32[]{:S(2)}, u32[]{:S(2)}) %collective-permute-start.1) | collective-permute-done | bytes 524320 | tf_op jit(solution)/shard_map/while/body/eval_jaxpr/ppermute | solution.py:16
  280.9 2.7 convolution_add_fusion.18
  283.6 5.2 collective-permute-start.1
  288.7 6.4 %collective-permute-done.1 = f32[8,128,128]{2,1,0:T(8,128)S(1)} collective-permute-done((f32[8,128,128]{2,1,0:T(8,128)}, f32[8,128,128]{2,1,0:T(8,128)S(1)}, u32[]{:S(2)}, u32[]{:S(2)}) %collective-permute-start.1) | collective-permute-done | bytes 524320 | tf_op jit(solution)/shard_map/while/body/eval_jaxpr/ppermute | solution.py:16
  295.2 2.7 convolution_add_fusion.18
  297.9 5.2 collective-permute-start.1
  303.0 6.4 %collective-permute-done.1 = f32[8,128,128]{2,1,0:T(8,128)S(1)} collective-permute-done((f32[8,128,128]{2,1,0:T(8,128)}, f32[8,128,128]{2,1,0:T(8,128)S(1)}, u32[]{:S(2)}, u32[]{:S(2)}) %collective-permute-start.1) | collective-permute-done | bytes 524320 | tf_op jit(solution)/shard_map/while/body/eval_jaxpr/ppermute | solution.py:16
  309.4 2.7 convolution_add_fusion.18
  312.1 5.2 collective-permute-start.1
  317.3 6.4 %collective-permute-done.1 = f32[8,128,128]{2,1,0:T(8,128)S(1)} collective-permute-done((f32[8,128,128]{2,1,0:T(8,128)}, f32[8,128,128]{2,1,0:T(8,128)S(1)}, u32[]{:S(2)}, u32[]{:S(2)}) %collective-permute-start.1) | collective-permute-done | bytes 524320 | tf_op jit(solution)/shard_map/while/body/eval_jaxpr/ppermute | solution.py:16
  328.0 12.6 %while.112 = (s32[]{:T(128)}, f32[8,128,128]{2,1,0:T(8,128)S(1)}, f32[2,8,128,128]{3,2,1,0:T(8,128)}, f32[2,8,128,1]{2,1,3,0:T(8,128)S(1)}, f32[2,8,128,128]{3,2...) while((s32[]{:T(128)}, f32[8,128,128]{2,1,0:T(8,128)S(1)}, ...), condition=%wide.region_12.13_spmd.clone, body=%wide.region_11.12_spmd.clone.sunk | while | flops 503922688 | bytes 22113312 | solution.py:163
  328.0 2.8 bitcast_dynamic-update-slice_fusion.11
  334.3 2.8 bitcast_dynamic-update-slice_fusion.11
  340.6 8.1 %while.115 = (s32[]{:T(128)}, f32[8,128,128]{2,1,0:T(8,128)}, f32[2,8,128,128]{3,2,1,0:T(8,128)}, f32[2,8,128,128]{3,2,1,0:T(8,128)}, s32[]{:T(128)}, /*index=5*/s32[]{:T(128)}) while((s32[]{:T(128)}, f32[8,128,128]{2,1,0:T(8,128)}, f32[2,8,128,128]{3,2,1,0:T(8,128)}, f32[2,8,128,128]{3,2,1,0:T(8,128)}, s32[]{:T(128)}, ...), condition=%wide.region_6.7_spmd.clone, body=%wide.region_5.6_spmd.clone.sunk | while | flops 201588736 | bytes 3147354 | solution.py:149
  341.7 3.0 convolution_add_fusion.22
  345.7 3.0 convolution_add_fusion.22
  349.7 100.7 %while.109 = (s32[]{:T(128)}, f32[8,128,128]{2,1,0:T(8,128)S(1)}, f32[8,128,128]{2,1,0:T(8,128)}, f32[8,128,128]{2,1,0:T(8,128)}, s32[]{:T(128)}) while((s32[]{:T(128)}, f32[8,128,128]{2,1,0:T(8,128)S(1)}, f32[8,128,128]{2,1,0:T(8,128)}, f32[8,128,128]{2,1,0:T(8,128)}, s32[]{:T(128)}) %tuple.197), condition=%wide.region_8.9_spmd, body=%wide.region_7.8_spmd.sunk | while | flops 201457664 | bytes 4194405 | solution.py:160
  349.8 2.6 convolution_add_fusion.17
  354.3 10.3 %collective-permute-done = f32[8,128,128]{2,1,0:T(8,128)S(1)} collective-permute-done((f32[8,128,128]{2,1,0:T(8,128)}, f32[8,128,128]{2,1,0:T(8,128)S(1)}, u32[]{:S(2)}, u32[]{:S(2)}) %collective-permute-start) | collective-permute-done | bytes 524320 | tf_op jit(solution)/shard_map/while/body/eval_jaxpr/ppermute | solution.py:16
  364.6 2.6 convolution_add_fusion.17
  369.2 9.7 %collective-permute-done = f32[8,128,128]{2,1,0:T(8,128)S(1)} collective-permute-done((f32[8,128,128]{2,1,0:T(8,128)}, f32[8,128,128]{2,1,0:T(8,128)S(1)}, u32[]{:S(2)}, u32[]{:S(2)}) %collective-permute-start) | collective-permute-done | bytes 524320 | tf_op jit(solution)/shard_map/while/body/eval_jaxpr/ppermute | solution.py:16
  378.9 2.6 convolution_add_fusion.17
  383.4 9.7 %collective-permute-done = f32[8,128,128]{2,1,0:T(8,128)S(1)} collective-permute-done((f32[8,128,128]{2,1,0:T(8,128)}, f32[8,128,128]{2,1,0:T(8,128)S(1)}, u32[]{:S(2)}, u32[]{:S(2)}) %collective-permute-start) | collective-permute-done | bytes 524320 | tf_op jit(solution)/shard_map/while/body/eval_jaxpr/ppermute | solution.py:16
  393.1 2.6 convolution_add_fusion.17
  397.7 9.7 %collective-permute-done = f32[8,128,128]{2,1,0:T(8,128)S(1)} collective-permute-done((f32[8,128,128]{2,1,0:T(8,128)}, f32[8,128,128]{2,1,0:T(8,128)S(1)}, u32[]{:S(2)}, u32[]{:S(2)}) %collective-permute-start) | collective-permute-done | bytes 524320 | tf_op jit(solution)/shard_map/while/body/eval_jaxpr/ppermute | solution.py:16
  407.3 2.6 convolution_add_fusion.17
  411.9 9.7 %collective-permute-done = f32[8,128,128]{2,1,0:T(8,128)S(1)} collective-permute-done((f32[8,128,128]{2,1,0:T(8,128)}, f32[8,128,128]{2,1,0:T(8,128)S(1)}, u32[]{:S(2)}, u32[]{:S(2)}) %collective-permute-start) | collective-permute-done | bytes 524320 | tf_op jit(solution)/shard_map/while/body/eval_jaxpr/ppermute | solution.py:16
  421.6 2.6 convolution_add_fusion.17
  426.1 9.7 %collective-permute-done = f32[8,128,128]{2,1,0:T(8,128)S(1)} collective-permute-done((f32[8,128,128]{2,1,0:T(8,128)}, f32[8,128,128]{2,1,0:T(8,128)S(1)}, u32[]{:S(2)}, u32[]{:S(2)}) %collective-permute-start) | collective-permute-done | bytes 524320 | tf_op jit(solution)/shard_map/while/body/eval_jaxpr/ppermute | solution.py:16
  435.8 2.6 convolution_add_fusion.17
  440.4 9.7 %collective-permute-done = f32[8,128,128]{2,1,0:T(8,128)S(1)} collective-permute-done((f32[8,128,128]{2,1,0:T(8,128)}, f32[8,128,128]{2,1,0:T(8,128)S(1)}, u32[]{:S(2)}, u32[]{:S(2)}) %collective-permute-start) | collective-permute-done | bytes 524320 | tf_op jit(solution)/shard_map/while/body/eval_jaxpr/ppermute | solution.py:16
  454.6 38.0 %while.113 = (s32[]{:T(128)}, f32[8,128,128]{2,1,0:T(8,128)S(1)}, f32[2,8,64,128]{3,2,1,0:T(8,128)}, f32[2,8,128,128]{3,2,1,0:T(8,128)}, f32[2,8,128]{2,1,0:T(8,...) while((s32[]{:T(128)}, f32[8,128,128]{2,1,0:T(8,128)S(1)}, ...), condition=%wide.region_15.16_spmd.clone, body=%wide.region_13.15_spmd.clone.sunk | while | flops 1411136512 | bytes 45981328 | solution.py:163
  454.6 2.8 fusion.255
  461.3 2.3 fusion.256
  473.5 2.8 fusion.255
  480.2 2.3 fusion.256
  492.6 2.8 copy.125
  495.4 3.8 fusion.121
  499.2 3.3 fusion.122
  506.8 3.1 convolution_add_fusion.10
  515.4 2.3 copy.131
  (239 shorter events, 109.8 us)
Async XLA Ops:
  7.2 178.4 %all-gather.2.cloned.1.call-start = ((), (), s32[]{:S(2)}) async-start(), calls=%async_computation | async-start | bytes 1310720 | tf_op jit(solution)/shard_map/all_gather | solution.py:81
  9.3 2.3 copy-start.12
  11.6 2.3 copy-start.32
  13.9 1.0 copy-start.22
  172.3 7.5 %copy-start.20 = (f32[16,1,128,128]{2,3,1,0:T(8,128)}, f32[16,1,128,128]{2,3,1,0:T(8,128)S(1)}, u32[]{:S(2)}) copy-start(f32[16,1,128,128]{2,3,1,0:T(8,128)S(1)} %custom-call.10) | copy-start | bytes 3145732
  172.3 3.3 copy-start.31
  183.0 1.4 copy-start.10
  196.0 1.8 copy-start.14
  197.2 4.6 copy-start.5
  198.9 1.0 copy-start.15
  203.8 1.8 copy-start.14
  205.0 4.6 copy-start.5
  206.7 1.0 copy-start.15
  211.6 1.0 copy-start
  212.6 3.7 copy-start.3
  218.9 3.7 copy-start.3
  227.9 10.1 %collective-permute-start.1 = (f32[8,128,128]{2,1,0:T(8,128)}, f32[8,128,128]{2,1,0:T(8,128)S(1)}, u32[]{:S(2)}, u32[]{:S(2)}) collective-permute-start(f32[8,128,128]{2,1,0:T(8,128)} %convolution_add_fusion.18), channel_id=1, source_target_pairs={{0,4},{4,8},{8,12},{12,16},{16,20},{20,24},{24,28},{1,5},{5,9},{9,... | collective-permute-start | bytes 1572872 | tf_op jit(solution)/shard_map/while/body/eval_jaxpr/ppermute | solution.py:16
  240.7 11.6 %collective-permute-start.1 = (f32[8,128,128]{2,1,0:T(8,128)}, f32[8,128,128]{2,1,0:T(8,128)S(1)}, u32[]{:S(2)}, u32[]{:S(2)}) collective-permute-start(f32[8,128,128]{2,1,0:T(8,128)} %convolution_add_fusion.18), channel_id=1, source_target_pairs={{0,4},{4,8},{8,12},{12,16},{16,20},{20,24},{24,28},{1,5},{5,9},{9,... | collective-permute-start | bytes 1572872 | tf_op jit(solution)/shard_map/while/body/eval_jaxpr/ppermute | solution.py:16
  255.0 11.6 %collective-permute-start.1 = (f32[8,128,128]{2,1,0:T(8,128)}, f32[8,128,128]{2,1,0:T(8,128)S(1)}, u32[]{:S(2)}, u32[]{:S(2)}) collective-permute-start(f32[8,128,128]{2,1,0:T(8,128)} %convolution_add_fusion.18), channel_id=1, source_target_pairs={{0,4},{4,8},{8,12},{12,16},{16,20},{20,24},{24,28},{1,5},{5,9},{9,... | collective-permute-start | bytes 1572872 | tf_op jit(solution)/shard_map/while/body/eval_jaxpr/ppermute | solution.py:16
  269.3 11.6 %collective-permute-start.1 = (f32[8,128,128]{2,1,0:T(8,128)}, f32[8,128,128]{2,1,0:T(8,128)S(1)}, u32[]{:S(2)}, u32[]{:S(2)}) collective-permute-start(f32[8,128,128]{2,1,0:T(8,128)} %convolution_add_fusion.18), channel_id=1, source_target_pairs={{0,4},{4,8},{8,12},{12,16},{16,20},{20,24},{24,28},{1,5},{5,9},{9,... | collective-permute-start | bytes 1572872 | tf_op jit(solution)/shard_map/while/body/eval_jaxpr/ppermute | solution.py:16
  283.6 11.6 %collective-permute-start.1 = (f32[8,128,128]{2,1,0:T(8,128)}, f32[8,128,128]{2,1,0:T(8,128)S(1)}, u32[]{:S(2)}, u32[]{:S(2)}) collective-permute-start(f32[8,128,128]{2,1,0:T(8,128)} %convolution_add_fusion.18), channel_id=1, source_target_pairs={{0,4},{4,8},{8,12},{12,16},{16,20},{20,24},{24,28},{1,5},{5,9},{9,... | collective-permute-start | bytes 1572872 | tf_op jit(solution)/shard_map/while/body/eval_jaxpr/ppermute | solution.py:16
  297.9 11.6 %collective-permute-start.1 = (f32[8,128,128]{2,1,0:T(8,128)}, f32[8,128,128]{2,1,0:T(8,128)S(1)}, u32[]{:S(2)}, u32[]{:S(2)}) collective-permute-start(f32[8,128,128]{2,1,0:T(8,128)} %convolution_add_fusion.18), channel_id=1, source_target_pairs={{0,4},{4,8},{8,12},{12,16},{16,20},{20,24},{24,28},{1,5},{5,9},{9,... | collective-permute-start | bytes 1572872 | tf_op jit(solution)/shard_map/while/body/eval_jaxpr/ppermute | solution.py:16
  312.1 11.6 %collective-permute-start.1 = (f32[8,128,128]{2,1,0:T(8,128)}, f32[8,128,128]{2,1,0:T(8,128)S(1)}, u32[]{:S(2)}, u32[]{:S(2)}) collective-permute-start(f32[8,128,128]{2,1,0:T(8,128)} %convolution_add_fusion.18), channel_id=1, source_target_pairs={{0,4},{4,8},{8,12},{12,16},{16,20},{20,24},{24,28},{1,5},{5,9},{9,... | collective-permute-start | bytes 1572872 | tf_op jit(solution)/shard_map/while/body/eval_jaxpr/ppermute | solution.py:16
  328.0 2.8 copy-start.6
  330.8 1.3 copy-start.1
  330.8 1.6 copy-start.24
  330.8 2.6 copy-start.7
  333.5 0.8 copy-start.25
  334.3 2.8 copy-start.6
  337.1 1.3 copy-start.1
  337.1 1.6 copy-start.24
  337.1 2.6 copy-start.7
  339.8 0.8 copy-start.25
  340.6 8.2 %copy-start.4 = (f32[8,128,128]{2,1,0:T(8,128)S(1)}, f32[8,128,128]{2,1,0:T(8,128)}, u32[]{:S(2)}) copy-start(f32[8,128,128]{2,1,0:T(8,128)} %get-tuple-element.1681) | copy-start | bytes 1572868
  352.4 12.2 %collective-permute-start = (f32[8,128,128]{2,1,0:T(8,128)}, f32[8,128,128]{2,1,0:T(8,128)S(1)}, u32[]{:S(2)}, u32[]{:S(2)}) collective-permute-start(f32[8,128,128]{2,1,0:T(8,128)} %convolution_add_fusion.17), channel_id=1, source_target_pairs={{4,0},{8,4},{12,8},{16,12},{20,16},{24,20},{28,24},{5,1},{9,5},{13... | collective-permute-start | bytes 1572872 | tf_op jit(solution)/shard_map/while/body/eval_jaxpr/ppermute | solution.py:16
  367.3 11.6 %collective-permute-start = (f32[8,128,128]{2,1,0:T(8,128)}, f32[8,128,128]{2,1,0:T(8,128)S(1)}, u32[]{:S(2)}, u32[]{:S(2)}) collective-permute-start(f32[8,128,128]{2,1,0:T(8,128)} %convolution_add_fusion.17), channel_id=1, source_target_pairs={{4,0},{8,4},{12,8},{16,12},{20,16},{24,20},{28,24},{5,1},{9,5},{13... | collective-permute-start | bytes 1572872 | tf_op jit(solution)/shard_map/while/body/eval_jaxpr/ppermute | solution.py:16
  381.5 11.6 %collective-permute-start = (f32[8,128,128]{2,1,0:T(8,128)}, f32[8,128,128]{2,1,0:T(8,128)S(1)}, u32[]{:S(2)}, u32[]{:S(2)}) collective-permute-start(f32[8,128,128]{2,1,0:T(8,128)} %convolution_add_fusion.17), channel_id=1, source_target_pairs={{4,0},{8,4},{12,8},{16,12},{20,16},{24,20},{28,24},{5,1},{9,5},{13... | collective-permute-start | bytes 1572872 | tf_op jit(solution)/shard_map/while/body/eval_jaxpr/ppermute | solution.py:16
  395.7 11.6 %collective-permute-start = (f32[8,128,128]{2,1,0:T(8,128)}, f32[8,128,128]{2,1,0:T(8,128)S(1)}, u32[]{:S(2)}, u32[]{:S(2)}) collective-permute-start(f32[8,128,128]{2,1,0:T(8,128)} %convolution_add_fusion.17), channel_id=1, source_target_pairs={{4,0},{8,4},{12,8},{16,12},{20,16},{24,20},{28,24},{5,1},{9,5},{13... | collective-permute-start | bytes 1572872 | tf_op jit(solution)/shard_map/while/body/eval_jaxpr/ppermute | solution.py:16
  410.0 11.6 %collective-permute-start = (f32[8,128,128]{2,1,0:T(8,128)}, f32[8,128,128]{2,1,0:T(8,128)S(1)}, u32[]{:S(2)}, u32[]{:S(2)}) collective-permute-start(f32[8,128,128]{2,1,0:T(8,128)} %convolution_add_fusion.17), channel_id=1, source_target_pairs={{4,0},{8,4},{12,8},{16,12},{20,16},{24,20},{28,24},{5,1},{9,5},{13... | collective-permute-start | bytes 1572872 | tf_op jit(solution)/shard_map/while/body/eval_jaxpr/ppermute | solution.py:16
  424.2 11.6 %collective-permute-start = (f32[8,128,128]{2,1,0:T(8,128)}, f32[8,128,128]{2,1,0:T(8,128)S(1)}, u32[]{:S(2)}, u32[]{:S(2)}) collective-permute-start(f32[8,128,128]{2,1,0:T(8,128)} %convolution_add_fusion.17), channel_id=1, source_target_pairs={{4,0},{8,4},{12,8},{16,12},{20,16},{24,20},{28,24},{5,1},{9,5},{13... | collective-permute-start | bytes 1572872 | tf_op jit(solution)/shard_map/while/body/eval_jaxpr/ppermute | solution.py:16
  438.5 11.6 %collective-permute-start = (f32[8,128,128]{2,1,0:T(8,128)}, f32[8,128,128]{2,1,0:T(8,128)S(1)}, u32[]{:S(2)}, u32[]{:S(2)}) collective-permute-start(f32[8,128,128]{2,1,0:T(8,128)} %convolution_add_fusion.17), channel_id=1, source_target_pairs={{4,0},{8,4},{12,8},{16,12},{20,16},{24,20},{28,24},{5,1},{9,5},{13... | collective-permute-start | bytes 1572872 | tf_op jit(solution)/shard_map/while/body/eval_jaxpr/ppermute | solution.py:16
  461.3 2.4 copy-start.9
  461.3 3.6 copy-start.2
  467.9 2.1 copy-start.26
  467.9 2.1 copy-start.8
  467.9 2.1 copy-start.16
  470.0 2.2 copy-start.27
  471.0 1.2 copy-start.17
  480.2 2.4 copy-start.9
  480.2 3.6 copy-start.2
  486.8 2.1 copy-start.26
  486.8 2.1 copy-start.8
  486.8 2.1 copy-start.16
  488.9 2.2 copy-start.27
  490.0 1.2 copy-start.17
  492.6 2.8 copy-start.11
  495.4 3.8 copy-start.18
  495.4 3.8 copy-start.19
  495.4 3.8 copy-start.21
  499.2 3.3 copy-start.23
  511.1 2.1 copy-start.13
  515.4 6.5 %copy-start.28 = (f32[2,128,1024]{2,1,0:T(8,128)S(1)}, f32[2,128,1024]{2,1,0:T(8,128)}, u32[]{:S(2)}) copy-start(f32[2,128,1024]{2,1,0:T(8,128)} %mul.236) | copy-start | bytes 3145732
  515.4 6.5 %copy-start.29 = (f32[2,128,1024]{2,1,0:T(8,128)S(1)}, f32[2,128,1024]{2,1,0:T(8,128)}, u32[]{:S(2)}) copy-start(f32[2,128,1024]{2,1,0:T(8,128)} %reshape.232) | copy-start | bytes 3145732
  519.8 2.1 copy-start.30
Sparse Core Ops, SparseCore 0:
  9.6 28.1 all-gather.1
where the time goes:
time: 540 us; the launch traced here: 530 us
  other arithmetic  164 us (30%)
  matrix products  131 us (24%)
  waiting for transfers between devices  114 us (21%)
  local copies, waits for them, and re-layouts  56.6 us (10%)
  starting transfers between devices  48.1 us (9%)
  between operations  14.7 us (3%)
    another operation x5, other arithmetic, block_solve(): jax.scipy.linalg.solve_triangular(system, joined, lower=True, unit_diagon...  157 us
    ppermute x14, waiting for transfers between devices, shifted(): return lax.ppermute(value, axis, pairs)  113 us
    dot_general x20, matrix products, matmul_heads(): return jnp.einsum('hij,hjk->hik', left, right, precision=highest)  53.6 us
    ppermute x14, starting transfers between devices, shifted(): return lax.ppermute(value, axis, pairs)  48 us
    another operation x11, local copies, waits for them, and re-layouts  11.7 us
    dot_general x6, matrix products, solved_step(): jnp.einsum('bik,biv->bkv', key_rows, weighted, precision=highest)  11.1 us
  transfers between devices with their start and end apart: 15, of which 14 were waited for; matrix products, arithmetic and copies ran while one was open for 33% of the time, Pallas kernels for 0%

commit v1 on v0

v1 whole, which is shorter than its diff:
```python
import functools

import jax
import jax.numpy as jnp
from jax import lax
from jax.experimental import pallas as pl
from jax.experimental.pallas import tpu as pltpu
from jax.sharding import PartitionSpec as P

HEAD_DIM = 128
MESH = pl.DeviceIdType.MESH
F32 = jnp.float32
BF16 = jnp.bfloat16


def product(left, right, over_left, over_right, passes=1):
    def one(a, b):
        return lax.dot_general(
            a, b, (((over_left,), (over_right,)), ((), ())), preferred_element_type=F32
        )

    left_high, right_high = left.astype(BF16), right.astype(BF16)
    if passes == 1:
        return one(left_high, right_high)
    total = one(left_high, right_high)
    if left.dtype == F32:
        total += one((left - left_high.astype(F32)).astype(BF16), right_high)
    if right.dtype == F32:
        total += one(left_high, (right - right_high.astype(F32)).astype(BF16))
    return total


def order(shape, axis, tokens, house):
    index = lax.broadcasted_iota(jnp.int32, shape, axis)
    return house * (index % tokens) + index // tokens


def inverse(strict_system, tokens, house, passes):
    shape = strict_system.shape
    row, column = order(shape, 0, tokens, house), order(shape, 1, tokens, house)
    result = jnp.where(row == column, 1.0, 0.0).astype(F32)
    size = 1
    while size < shape[0]:
        joins = (row // (2 * size) == column // (2 * size)) & (row // size != column // size)
        corner = jnp.where(joins, strict_system, 0.0)
        if size == 1:
            result = result - corner
        else:
            half = product(corner, result, 1, 0, passes)
            result = result - product(result, half, 1, 0, passes)
        size *= 2
    return result


def normalize(raw):
    raw = raw.astype(F32)
    scaling = lax.rsqrt(jnp.sum(raw * raw, axis=-1, keepdims=True) + 1e-06)
    return raw * scaling, scaling


def read_mask(tokens, rows):
    reader = lax.broadcasted_iota(jnp.int32, (tokens, rows), 0)
    return lax.broadcasted_iota(jnp.int32, (tokens, rows), 1) % tokens <= reader


def solve_part(query, raw, value, rate, house, inv_passes=3, passes=3):
    tokens = query.shape[0]
    rows = raw.shape[0]
    query = query.astype(F32) * HEAD_DIM ** (-0.5)
    key, _ = normalize(raw)
    gram = product(key, key, 1, 1, inv_passes)
    shape = (rows, rows)
    before = order(shape, 1, tokens, house) < order(shape, 0, tokens, house)
    gram = jnp.where(before, gram, 0.0)
    solver = inverse(gram * rate, tokens, house, inv_passes)
    solved_k = product(solver, key * rate, 1, 0, passes)
    solved_v = product(solver, value.astype(F32) * rate, 1, 0, passes)
    decay = product(key, solved_k, 0, 0, passes)
    offset = product(key, solved_v, 0, 0, passes)
    scores = jnp.where(read_mask(tokens, rows), product(query, key, 1, 1, passes), 0.0)
    reading = query - product(scores, solved_k, 1, 0, passes)
    return gram, solver, solved_k, solved_v, decay, offset, scores, reading


def final_part(
    query, raw, value, rate, gram, solver, solved_k, solved_v, scores, grad, state, adjoint, passes=3
):
    house = raw.shape[0] // query.shape[0]
    tokens = query.shape[0]
    rows = raw.shape[0]
    query = query.astype(F32) * HEAD_DIM ** (-0.5)
    key, scaling = normalize(raw)
    weighted = product(solved_k, state, 1, 0, passes) - solved_v
    errors = product(key, state, 1, 0, passes) - value.astype(F32)
    errors = errors - product(gram, weighted, 1, 0, passes)
    grad_weighted = -product(scores, grad, 0, 0, passes) - product(key, adjoint, 1, 0, passes)
    unscaled = product(solver, grad_weighted, 0, 0, passes)
    pulled = unscaled * rate
    grad_rate = jnp.sum(errors * unscaled, axis=1, keepdims=True)
    grad_scores = -jnp.where(read_mask(tokens, rows), product(grad, weighted, 1, 1, passes), 0.0)
    grad_query = product(grad, state, 1, 1, passes) + product(grad_scores, key, 1, 0, passes)
    shape = (rows, rows)
    before = order(shape, 1, tokens, house) < order(shape, 0, tokens, house)
    grad_gram = -jnp.where(before, product(pulled, weighted, 1, 1, passes), 0.0)
    grad_key = (
        product(grad_scores, query, 0, 0, passes)
        - product(weighted, adjoint, 1, 1, passes)
        + product(pulled, state, 1, 1, passes)
        + product(grad_gram, key, 1, 0, passes)
        + product(grad_gram, key, 0, 0, passes)
    )
    along = jnp.sum(grad_key * key, axis=1, keepdims=True)
    grad_raw = scaling * (grad_key - key * along)
    return grad_query * HEAD_DIM ** (-0.5), grad_raw, -pulled, grad_rate


def kernel(
    ctx_count,
    head_count,
    query_ref, raw_ref, value_ref, rate_ref, grad_ref, weight_ref,
    out_query, out_key, out_value, out_rate,
    weight, gathered, rates, grad_rates, grads,
    gram, solver, solved_k, solved_v, decay, offset, scores, reading, local_grad,
    state, state_out, adjoint, adjoint_out,
    weight_sem, up_send, down_send, gather_recv, state_send, state_recv, adjoint_send, adjoint_recv,
):
    me, column = lax.axis_index("ctx"), lax.axis_index("head")
    house, tokens = raw_ref.shape[0], raw_ref.shape[1]
    heads = state.shape[0]
    shard = grad_ref.shape[0]
    rows = house * tokens

    weight_copy = pltpu.make_async_copy(weight_ref, weight, weight_sem)
    weight_copy.start()

    barrier = pltpu.get_barrier_semaphore()
    neighbours = (
        (me > 0, {"ctx": me - 1}),
        (me < ctx_count - 1, {"ctx": me + 1}),
        (column > 0, {"head": column - 1}),
        (column < head_count - 1, {"head": column + 1}),
    )
    for there, device in neighbours:
        @pl.when(there)
        def _():
            pl.semaphore_signal(barrier, inc=1, device_id=device, device_id_type=MESH)
    pl.semaphore_wait(barrier, sum(there.astype(jnp.int32) for there, _ in neighbours))

    def slot(owner):
        return gathered.at[pl.ds(pl.multiple_of(owner * shard, shard), shard)]

    def passing(owner, up):
        return pltpu.make_async_remote_copy(
            src_ref=slot(owner),
            dst_ref=slot(owner),
            send_sem=(up_send if up else down_send).at[owner],
            recv_sem=gather_recv.at[owner],
            device_id={"head": lax.rem(column + (1 if up else head_count - 1), head_count)},
            device_id_type=MESH,
        )

    gathered[pl.ds(pl.multiple_of(column * shard, shard), shard)] = grad_ref[...]

    def send_on(owner, up):
        @pl.when(column < head_count - 1 if up else column > 0)
        def _():
            passing(owner, up).start()

    send_on(column, True)
    send_on(column, False)

    rates[...] = jnp.zeros_like(rates)
    grad_rates[...] = jnp.zeros_like(grad_rates)
    rates[pl.ds(0, house * heads)] = rate_ref[...]
    rates[...] = jnp.transpose(rates[...])

    lanes = lax.broadcasted_iota(jnp.int32, (tokens, tokens), 1)

    def rate_of(head):
        parts = [
            jnp.sum(jnp.where(lanes == head * house + j, rates[...], 0.0), axis=1, keepdims=True)
            for j in range(house)
        ]
        return jnp.concatenate(parts, axis=0)

    def columns(head):
        return pl.ds(pl.multiple_of(head * HEAD_DIM, HEAD_DIM), HEAD_DIM)

    def load(ref, head):
        return ref[:, :, columns(head)].reshape(rows, HEAD_DIM)

    def solve_head(head):
        results = solve_part(
            query_ref[:, columns(head)], load(raw_ref, head), load(value_ref, head), rate_of(head), house
        )
        kept = (gram, solver, solved_k, solved_v, decay, offset, scores, reading)
        for ref, result in zip(kept, results):
            ref[head] = result.astype(ref.dtype)

    together = 2 if heads % 2 == 0 else 1
    turns = heads // together

    def gather_turn(turn):
        for owner, up in ((column - turn, True), (column + turn, False)):
            @pl.when((owner >= 0) & (owner < head_count))
            def _():
                passing(owner, up).wait_recv()
                send_on(owner, up)

    def solve_turn(turn, carry):
        for part in range(together):
            solve_head(turn * together + part)

        @pl.when((turn + 1) < head_count)
        def _():
            gather_turn(turn + 1)

        return carry

    lax.fori_loop(0, turns, solve_turn, 0)
    for turn in range(turns + 1, head_count):
        gather_turn(turn)

    @pl.when(me == 0)
    def _():
        state[...] = jnp.zeros_like(state)

    @pl.when(me == ctx_count - 1)
    def _():
        adjoint[...] = jnp.zeros_like(adjoint)

    weight_copy.wait()

    def grad_turn(turn, carry):
        part = pl.ds(pl.multiple_of(turn * together * HEAD_DIM, HEAD_DIM), together * HEAD_DIM)
        block = product(gathered[...], weight[part, :], 1, 1).astype(BF16)
        for index in range(together):
            head = turn * together + index
            grad = block[:, index * HEAD_DIM : (index + 1) * HEAD_DIM]
            grads[head] = grad
            local_grad[head] = product(reading[head], grad, 0, 0)
        return carry

    lax.fori_loop(0, turns, grad_turn, 0)

    def state_copy(head):
        return pltpu.make_async_remote_copy(
            src_ref=state_out.at[head], dst_ref=state.at[head],
            send_sem=state_send.at[head], recv_sem=state_recv.at[head],
            device_id={"ctx": lax.rem(me + 1, ctx_count)}, device_id_type=MESH,
        )

    def adjoint_copy(head):
        return pltpu.make_async_remote_copy(
            src_ref=adjoint_out.at[head], dst_ref=adjoint.at[head],
            send_sem=adjoint_send.at[head], recv_sem=adjoint_recv.at[head],
            device_id={"ctx": lax.rem(me + ctx_count - 1, ctx_count)}, device_id_type=MESH,
        )

    far = ctx_count - 1 - me

    def wave(step, carry):
        head_f = step - me

        @pl.when((head_f >= 0) & (head_f < heads))
        def _():
            @pl.when(me > 0)
            def _():
                state_copy(head_f).wait_recv()

            @pl.when(far > 0)
            def _():
                held = state[head_f]
                state_out[head_f] = held + offset[head_f] - product(decay[head_f], held, 1, 0)
                state_copy(head_f).start()

        head_b = step - far

        @pl.when((head_b >= 0) & (head_b < heads))
        def _():
            @pl.when(far > 0)
            def _():
                adjoint_copy(head_b).wait_recv()

            @pl.when(me > 0)
            def _():
                held = adjoint[head_b]
                adjoint_out[head_b] = held + local_grad[head_b] - product(decay[head_b], held, 0, 0)
                adjoint_copy(head_b).start()

        head = step - jnp.maximum(me, far)

        @pl.when((head >= 0) & (head < heads))
        def _():
            grad_query, grad_raw, grad_value, grad_rate = final_part(
                query_ref[:, columns(head)], load(raw_ref, head), load(value_ref, head), rate_of(head),
                gram[head], solver[head], solved_k[head], solved_v[head], scores[head],
                grads[head], state[head], adjoint[head],
            )
            out_query[:, columns(head)] = grad_query.astype(BF16)
            out_key[:, :, columns(head)] = grad_raw.reshape(house, tokens, HEAD_DIM).astype(BF16)
            out_value[:, :, columns(head)] = grad_value.reshape(house, tokens, HEAD_DIM).astype(BF16)
            total = grad_rates[...]
            for j in range(house):
                total = jnp.where(
                    lanes == head * house + j, grad_rate[j * tokens : (j + 1) * tokens], total
                )
            grad_rates[...] = total

        return carry

    lax.fori_loop(0, ctx_count - 1 + heads, wave, 0)

    out_rate[...] = jnp.transpose(grad_rates[...])[: house * heads]

    def finish(head, carry):
        @pl.when(far > 0)
        def _():
            state_copy(head).wait_send()

        @pl.when(me > 0)
        def _():
            adjoint_copy(head).wait_send()

        return carry

    lax.fori_loop(0, heads, finish, 0)
    for owner in range(head_count):
        @pl.when((owner <= column) & (column < head_count - 1))
        def _():
            passing(owner, True).wait_send()

        @pl.when((owner >= column) & (column > 0))
        def _():
            passing(owner, False).wait_send()


def shards(queries, key_input, value_input, beta_rates, out_grad, out_weight):
    house, tokens, width = key_input.shape
    heads = width // HEAD_DIM
    rows = house * tokens
    ctx_count, head_count = lax.axis_size("ctx"), lax.axis_size("head")
    vmem = pl.BlockSpec(memory_space=pltpu.VMEM)

    def held(*shape, dtype=F32):
        return pltpu.VMEM((heads,) + shape, dtype)

    results = pl.pallas_call(
        functools.partial(kernel, ctx_count, head_count),
        out_shape=(
            jax.ShapeDtypeStruct(queries.shape, BF16),
            jax.ShapeDtypeStruct(key_input.shape, BF16),
            jax.ShapeDtypeStruct(value_input.shape, BF16),
            jax.ShapeDtypeStruct((heads * house, tokens), F32),
        ),
        in_specs=[vmem] * 5 + [pl.BlockSpec(memory_space=pl.ANY)],
        out_specs=(vmem,) * 4,
        scratch_shapes=[
            pltpu.VMEM(out_weight.shape, BF16),
            pltpu.VMEM((tokens, out_grad.shape[1]), BF16),
            pltpu.VMEM((tokens, tokens), F32),
            pltpu.VMEM((tokens, tokens), F32),
            held(tokens, HEAD_DIM, dtype=BF16),
            held(rows, rows, dtype=BF16),
            held(rows, rows, dtype=BF16),
            held(rows, HEAD_DIM),
            held(rows, HEAD_DIM),
            held(HEAD_DIM, HEAD_DIM, dtype=BF16),
            held(HEAD_DIM, HEAD_DIM),
            held(tokens, rows, dtype=BF16),
            held(tokens, HEAD_DIM, dtype=BF16),
            held(HEAD_DIM, HEAD_DIM),
            held(HEAD_DIM, HEAD_DIM),
            held(HEAD_DIM, HEAD_DIM),
            held(HEAD_DIM, HEAD_DIM),
            held(HEAD_DIM, HEAD_DIM),
            pltpu.SemaphoreType.DMA,
            pltpu.SemaphoreType.DMA((head_count,)),
            pltpu.SemaphoreType.DMA((head_count,)),
            pltpu.SemaphoreType.DMA((head_count,)),
            pltpu.SemaphoreType.DMA((heads,)),
            pltpu.SemaphoreType.DMA((heads,)),
            pltpu.SemaphoreType.DMA((heads,)),
            pltpu.SemaphoreType.DMA((heads,)),
        ],
        compiler_params=pltpu.CompilerParams(
            collective_id=0, has_side_effects=True, vmem_limit_bytes=56 * 1024 * 1024
        ),
    )(
        queries,
        key_input,
        value_input,
        beta_rates.reshape(heads * house, tokens),
        out_grad,
        out_weight,
    )
    return results[:3] + (results[3].reshape(beta_rates.shape),)


def solution(mesh):
    placed = (
        P("ctx", "head"),
        P(None, "ctx", "head"),
        P(None, "ctx", "head"),
        P("head", None, "ctx"),
        P(("ctx", "head"), None),
        P("head", None),
    )
    return jax.shard_map(
        shards,
        mesh=mesh,
        in_specs=placed,
        out_specs=placed[:4],
        check_vma=False,
    )
```

time: 540 us -> 102 us (0.19)
  the two profiles are of different devices: /device:TPU:19 before, /device:TPU:0 now
where the time goes in v1:
time: 102 us
  Pallas kernels  94.2 us (92%)
  local copies, waits for them, and re-layouts  6.7 us (7%)
    pallas_call x1, Pallas kernels, shards(): pl.pallas_call(functools.partial(kernel, ctx_count, head_count), out_shap...  94.2 us
    unnamed x4, local copies, waits for them, and re-layouts  6.7 us

profile of v1, /device:TPU:0, one launch (start us, length us, event | category | flops | bytes accessed | tf_op | source)
XLA Modules:
  0.0 101.6 jit_solution(18041261881928505315)
XLA Ops:
  0.6 94.2 %shard_map.93 = (bf16[128,1024]{1,0:T(8,128)(2,1)}, bf16[2,128,1024]{2,1,0:T(8,128)(2,1)}, bf16[2,128,1024]{2,1,0:T(8,128)(2,1)}, f32[16,128]{1,0:T(8,128)}) custom-call(bf16[128,1024]{1,0:T(8,128)(2,1)} %query_ref.1, bf16[2,128,1024]{2,1,0:T(8,128)(2,1)} %raw_ref.1, bf16[2,128,1024]{2,1,0:T(8,128)(2,1)} %value_ref.1, f32[16,128]{1,0:T(8,128)} %bitcast.3, ...), custom_call_target="tpu_custom_call" | custom-call | tf_op jit(solution)/shard_map/pallas_call | solution.py:348
  94.9 1.7 %copy.14 = bf16[128,1024]{1,0:T(8,128)(2,1)} copy(bf16[128,1024]{1,0:T(8,128)(2,1)} %get-tuple-element.16) | data formatting | bytes 524288
  96.5 1.9 %copy.15 = bf16[2,128,1024]{2,1,0:T(8,128)(2,1)} copy(bf16[2,128,1024]{2,1,0:T(8,128)(2,1)} %get-tuple-element.17) | data formatting | bytes 1048576
  98.4 1.9 %copy.16 = bf16[2,128,1024]{2,1,0:T(8,128)(2,1)} copy(bf16[2,128,1024]{2,1,0:T(8,128)(2,1)} %get-tuple-element.18) | data formatting | bytes 1048576
  100.3 1.3 %copy.17 = f32[8,2,128]{2,1,0:T(2,128)} copy(f32[8,2,128]{2,1,0:T(2,128)} %bitcast.2) | data formatting | bytes 16384

commit v2 on v1

v2 whole, which is shorter than its diff:
```python
import functools

import jax
import jax.numpy as jnp
from jax import lax
from jax.experimental import pallas as pl
from jax.experimental.pallas import tpu as pltpu
from jax.sharding import PartitionSpec as P

HEAD_DIM = 128
MESH = pl.DeviceIdType.MESH
F32 = jnp.float32
BF16 = jnp.bfloat16
SOLVER = BF16
SPLIT = {
    "gram": "lr", "inv1": "lr", "inv2": "lr", "sk": "lr", "sv": "lr", "dec": "lr", "off": "lr", "sc": "lr", "rd": "lr", "w": "lr",
    "gw1": "lr", "gs": "lr", "q2": "lr", "k1": "lr", "gw2": "lr", "un": "lr", "gg": "lr", "k2": "lr", "k4": "lr",
}


def product(left, right, over_left, over_right, split=""):
    def one(a, b):
        return lax.dot_general(
            a, b, (((over_left,), (over_right,)), ((), ())), preferred_element_type=F32
        )

    left_high, right_high = left.astype(BF16), right.astype(BF16)
    total = one(left_high, right_high)
    if "l" in split and left.dtype == F32:
        total += one((left - left_high.astype(F32)).astype(BF16), right_high)
    if "r" in split and right.dtype == F32:
        total += one(left_high, (right - right_high.astype(F32)).astype(BF16))
    return total


def order(shape, axis, tokens, house):
    index = lax.broadcasted_iota(jnp.int32, shape, axis)
    return house * (index % tokens) + index // tokens


def inverse(strict_system, tokens, house):
    shape = strict_system.shape
    row, column = order(shape, 0, tokens, house), order(shape, 1, tokens, house)
    result = jnp.where(row == column, 1.0, 0.0).astype(F32)
    size = 1
    while size < shape[0]:
        joins = (row // (2 * size) == column // (2 * size)) & (row // size != column // size)
        corner = jnp.where(joins, strict_system, 0.0)
        if size == 1:
            result = result - corner
        else:
            half = product(corner, result, 1, 0, SPLIT["inv1"])
            result = result - product(result, half, 1, 0, SPLIT["inv2"])
        size *= 2
    return result


def normalize(raw):
    raw = raw.astype(F32)
    scaling = lax.rsqrt(jnp.sum(raw * raw, axis=-1, keepdims=True) + 1e-06)
    return raw * scaling, scaling


def read_mask(tokens, rows):
    reader = lax.broadcasted_iota(jnp.int32, (tokens, rows), 0)
    return lax.broadcasted_iota(jnp.int32, (tokens, rows), 1) % tokens <= reader


def strict_mask(tokens, house):
    shape = (house * tokens, house * tokens)
    return order(shape, 1, tokens, house) < order(shape, 0, tokens, house)


def solve_part(query, raw, value, rate, house):
    tokens = query.shape[0]
    query = query.astype(F32) * HEAD_DIM ** (-0.5)
    key, _ = normalize(raw)
    gram = product(key, key, 1, 1, SPLIT["gram"])
    gram = jnp.where(strict_mask(tokens, house), gram, 0.0)
    solver = inverse(gram * rate, tokens, house)
    solved_k = product(solver, key * rate, 1, 0, SPLIT["sk"])
    solved_v = product(solver, value.astype(F32) * rate, 1, 0, SPLIT["sv"])
    decay = product(key, solved_k, 0, 0, SPLIT["dec"])
    offset = product(key, solved_v, 0, 0, SPLIT["off"])
    scores = jnp.where(read_mask(tokens, gram.shape[0]), product(query, key, 1, 1, SPLIT["sc"]), 0.0)
    reading = query - product(scores, solved_k, 1, 0, SPLIT["rd"])
    return gram, solver, solved_k, solved_v, decay, offset, scores, reading


def early_part(query, raw, value, gram, solved_k, solved_v, scores, grad, state):
    tokens = query.shape[0]
    query = query.astype(F32) * HEAD_DIM ** (-0.5)
    key, _ = normalize(raw)
    weighted = product(solved_k, state, 1, 0, SPLIT["w"]) - solved_v
    errors = product(key, state, 1, 0) - value.astype(F32) - product(gram, weighted, 1, 0)
    grad_weighted = -product(scores, grad, 0, 0, SPLIT["gw1"])
    grad_scores = product(grad, weighted, 1, 1, SPLIT["gs"])
    grad_scores = jnp.where(read_mask(tokens, raw.shape[0]), -grad_scores, 0.0)
    grad_query = product(grad, state, 1, 1, "r") + product(grad_scores, key, 1, 0, SPLIT["q2"])
    grad_key = product(grad_scores, query, 0, 0, SPLIT["k1"])
    return weighted, errors, grad_weighted, grad_query * HEAD_DIM ** (-0.5), grad_key


def late_part(raw, rate, solver, weighted, errors, grad_weighted, grad_key, state, adjoint, house):
    tokens = raw.shape[0] // house
    key, scaling = normalize(raw)
    grad_weighted = grad_weighted - product(key, adjoint, 1, 0, SPLIT["gw2"])
    unscaled = product(solver, grad_weighted, 0, 0, SPLIT["un"])
    pulled = unscaled * rate
    grad_rate = jnp.sum(errors * unscaled, axis=1, keepdims=True)
    grad_gram = -jnp.where(strict_mask(tokens, house), product(pulled, weighted, 1, 1, SPLIT["gg"]), 0.0)
    grad_key = (
        grad_key
        - product(weighted, adjoint, 1, 1, SPLIT["k2"])
        + product(pulled, state, 1, 1, SPLIT["k2"])
        + product(grad_gram, key, 1, 0, SPLIT["k4"])
        + product(grad_gram, key, 0, 0, SPLIT["k4"])
    )
    along = jnp.sum(grad_key * key, axis=1, keepdims=True)
    grad_raw = scaling * (grad_key - key * along)
    return grad_raw, -pulled, grad_rate


def kernel(
    ctx_count,
    head_count,
    query_ref, raw_ref, value_ref, rate_ref, grad_ref, weight_ref,
    out_query, out_key, out_value, out_rate,
    weight, gathered, rates, grads,
    gram, solver, solved_k, solved_v, decay, offset, scores, reading, local_grad,
    errors, grad_weighted, grad_key, state, adjoint,
    decay_in, offset_in, grad_in, states, adjoints,
    weight_sem, up_send, down_send, gather_recv,
    decay_send, decay_recv, offset_send, offset_recv, grad_send, grad_recv,
    state_send, state_recv, adjoint_send, adjoint_recv,
):
    me, column = lax.axis_index("ctx"), lax.axis_index("head")
    house, tokens = raw_ref.shape[0], raw_ref.shape[1]
    heads = state.shape[0]
    shard = grad_ref.shape[0]
    rows = house * tokens
    spacing = ctx_count // heads
    owns = lax.rem(me, spacing) == 0
    mine = me // spacing

    weight_copy = pltpu.make_async_copy(weight_ref, weight, weight_sem)
    weight_copy.start()

    barrier = pltpu.get_barrier_semaphore()

    def greet(there, device):
        @pl.when(there)
        def _():
            pl.semaphore_signal(barrier, inc=1, device_id=device, device_id_type=MESH)

        return there.astype(jnp.int32)

    peers = greet(column > 0, {"head": column - 1})
    peers += greet(column < head_count - 1, {"head": column + 1})
    for other in range(ctx_count):
        meets = (me != other) if other % spacing == 0 else (me != other) & owns
        peers += greet(meets, {"ctx": other})
    pl.semaphore_wait(barrier, peers)

    def slot(owner):
        return gathered.at[pl.ds(pl.multiple_of(owner * shard, shard), shard)]

    def passing(owner, up):
        return pltpu.make_async_remote_copy(
            src_ref=slot(owner),
            dst_ref=slot(owner),
            send_sem=(up_send if up else down_send).at[owner],
            recv_sem=gather_recv.at[owner],
            device_id={"head": lax.rem(column + (1 if up else head_count - 1), head_count)},
            device_id_type=MESH,
        )

    gathered[pl.ds(pl.multiple_of(column * shard, shard), shard)] = grad_ref[...]

    def send_on(owner, up):
        @pl.when(column < head_count - 1 if up else column > 0)
        def _():
            passing(owner, up).start()

    send_on(column, True)
    send_on(column, False)

    rates[...] = jnp.zeros_like(rates)
    rates[pl.ds(0, house * heads)] = rate_ref[...]
    rates[...] = jnp.transpose(rates[...])

    lanes = lax.broadcasted_iota(jnp.int32, (tokens, tokens), 1)

    def rate_of(head):
        parts = [
            jnp.sum(jnp.where(lanes == head * house + j, rates[...], 0.0), axis=1, keepdims=True)
            for j in range(house)
        ]
        return jnp.concatenate(parts, axis=0)

    def columns(head):
        return pl.ds(pl.multiple_of(head * HEAD_DIM, HEAD_DIM), HEAD_DIM)

    def load(ref, head):
        return ref[:, :, columns(head)].reshape(rows, HEAD_DIM)

    def to_owner(kept, landing, send, recv, head, source):
        return pltpu.make_async_remote_copy(
            src_ref=kept.at[head], dst_ref=landing.at[source], send_sem=send.at[head],
            recv_sem=recv.at[source], device_id={"ctx": head * spacing}, device_id_type=MESH,
        )

    def give(kept, landing, send, recv, head):
        away = me != head * spacing

        @pl.when(away)
        def _():
            to_owner(kept, landing, send, recv, head, me).start()

        @pl.when(jnp.logical_not(away))
        def _():
            landing[me] = kept[head]

    decay_args = (decay, decay_in, decay_send, decay_recv)
    offset_args = (offset, offset_in, offset_send, offset_recv)
    grad_args = (local_grad, grad_in, grad_send, grad_recv)

    def to_user(made, landing, send, recv, user, head):
        return pltpu.make_async_remote_copy(
            src_ref=made.at[user], dst_ref=landing.at[head], send_sem=send.at[user],
            recv_sem=recv.at[head], device_id={"ctx": user}, device_id_type=MESH,
        )

    def hand_out(made, landing, send, recv, user):
        @pl.when(me != user)
        def _():
            to_user(made, landing, send, recv, user, mine).start()

        @pl.when(me == user)
        def _():
            landing[mine] = made[user]

    state_args = (states, state, state_send, state_recv)
    adjoint_args = (adjoints, adjoint, adjoint_send, adjoint_recv)

    def solve_head(head):
        results = solve_part(
            query_ref[:, columns(head)], load(raw_ref, head), load(value_ref, head), rate_of(head), house
        )
        kept = (gram, solver, solved_k, solved_v, decay, offset, scores, reading)
        for ref, result in zip(kept, results):
            ref[head] = result.astype(ref.dtype)

    together = 2 if heads % 2 == 0 else 1
    turns = heads // together

    def gather_turn(turn):
        for owner, up in ((column - turn, True), (column + turn, False)):
            @pl.when((owner >= 0) & (owner < head_count))
            def _():
                passing(owner, up).wait_recv()
                send_on(owner, up)

    def solve_turn(turn, carry):
        for part in range(together):
            solve_head(turn * together + part)
        for part in range(together):
            give(*decay_args, turn * together + part)
            give(*offset_args, turn * together + part)

        @pl.when((turn + 1) < head_count)
        def _():
            gather_turn(turn + 1)

        return carry

    lax.fori_loop(0, turns, solve_turn, 0)
    for turn in range(turns + 1, head_count):
        gather_turn(turn)

    weight_copy.wait()

    def grad_turn(turn, carry):
        part = pl.ds(pl.multiple_of(turn * together * HEAD_DIM, HEAD_DIM), together * HEAD_DIM)
        block = product(gathered[...], weight[part, :], 1, 1).astype(BF16)
        for index in range(together):
            head = turn * together + index
            grad = block[:, index * HEAD_DIM : (index + 1) * HEAD_DIM]
            grads[head] = grad
            local_grad[head] = product(reading[head], grad, 0, 0)
            give(*grad_args, head)
        return carry

    lax.fori_loop(0, turns, grad_turn, 0)

    @pl.when(owns)
    def _():
        def arrive(args, source):
            @pl.when(me != source)
            def _():
                to_owner(*args, mine, source).wait_recv()

        def forward(user, held):
            states[user] = held
            hand_out(*state_args, user)
            arrive(decay_args, user)
            arrive(offset_args, user)
            return held + offset_in[user] - product(decay_in[user], held, 1, 0)

        zero = jnp.zeros((HEAD_DIM, HEAD_DIM), F32)
        lax.fori_loop(0, ctx_count, forward, zero)

        def backward(step, held):
            user = ctx_count - 1 - step
            adjoints[user] = held
            hand_out(*adjoint_args, user)
            arrive(grad_args, user)
            return held + grad_in[user] - product(decay_in[user], held, 0, 0)

        lax.fori_loop(0, ctx_count, backward, zero)

    def early_head(head):
        @pl.when(me != head * spacing)
        def _():
            to_user(*state_args, me, head).wait_recv()

    def early_turn(turn, carry):
        for part in range(together):
            early_head(turn * together + part)
        for part in range(together):
            head = turn * together + part
            results = early_part(
                query_ref[:, columns(head)], load(raw_ref, head), load(value_ref, head), gram[head],
                solved_k[head], solved_v[head], scores[head], grads[head], state[head],
            )
            solved_v[head], errors[head], grad_weighted[head] = results[:3]
            out_query[:, columns(head)] = results[3].astype(BF16)
            grad_key[head] = results[4]
        return carry

    lax.fori_loop(0, turns, early_turn, 0)

    def late_turn(turn, total):
        for part in range(together):
            head = turn * together + part

            @pl.when(me != head * spacing)
            def _():
                to_user(*adjoint_args, me, head).wait_recv()

        for part in range(together):
            head = turn * together + part
            grad_raw, grad_value, grad_rate = late_part(
                load(raw_ref, head), rate_of(head), solver[head], solved_v[head], errors[head],
                grad_weighted[head], grad_key[head], state[head], adjoint[head], house,
            )
            out_key[:, :, columns(head)] = grad_raw.reshape(house, tokens, HEAD_DIM).astype(BF16)
            out_value[:, :, columns(head)] = grad_value.reshape(house, tokens, HEAD_DIM).astype(BF16)
            for j in range(house):
                total = jnp.where(
                    lanes == head * house + j, grad_rate[j * tokens : (j + 1) * tokens], total
                )
        return total

    total = lax.fori_loop(0, turns, late_turn, jnp.zeros((tokens, tokens), F32))
    out_rate[...] = jnp.transpose(total)[: house * heads]

    def given(head, carry):
        @pl.when(me != head * spacing)
        def _():
            for args in (decay_args, offset_args, grad_args):
                to_owner(*args, head, me).wait_send()

        return carry

    lax.fori_loop(0, heads, given, 0)

    def handed(user, carry):
        @pl.when(owns & (me != user))
        def _():
            for args in (state_args, adjoint_args):
                to_user(*args, user, mine).wait_send()

        return carry

    lax.fori_loop(0, ctx_count, handed, 0)
    for owner in range(head_count):
        @pl.when((owner <= column) & (column < head_count - 1))
        def _():
            passing(owner, True).wait_send()

        @pl.when((owner >= column) & (column > 0))
        def _():
            passing(owner, False).wait_send()


def shards(queries, key_input, value_input, beta_rates, out_grad, out_weight):
    house, tokens, width = key_input.shape
    heads = width // HEAD_DIM
    rows = house * tokens
    square = (HEAD_DIM, HEAD_DIM)
    ctx_count, head_count = lax.axis_size("ctx"), lax.axis_size("head")
    vmem = pl.BlockSpec(memory_space=pltpu.VMEM)

    def held(*shape, dtype=F32):
        return pltpu.VMEM((heads,) + shape, dtype)

    results = pl.pallas_call(
        functools.partial(kernel, ctx_count, head_count),
        out_shape=(
            jax.ShapeDtypeStruct(queries.shape, BF16),
            jax.ShapeDtypeStruct(key_input.shape, BF16),
            jax.ShapeDtypeStruct(value_input.shape, BF16),
            jax.ShapeDtypeStruct((heads * house, tokens), F32),
        ),
        in_specs=[vmem] * 5 + [pl.BlockSpec(memory_space=pl.ANY)],
        out_specs=(vmem,) * 4,
        scratch_shapes=[
            pltpu.VMEM(out_weight.shape, BF16),
            pltpu.VMEM((tokens, out_grad.shape[1]), BF16),
            pltpu.VMEM((tokens, tokens), F32),
            held(tokens, HEAD_DIM, dtype=BF16),
            held(rows, rows, dtype=BF16),
            held(rows, rows, dtype=SOLVER),
            held(rows, HEAD_DIM),
            held(rows, HEAD_DIM),
            held(*square, dtype=BF16),
            held(*square),
            held(tokens, rows, dtype=BF16),
            held(tokens, HEAD_DIM, dtype=BF16),
            held(*square),
            held(rows, HEAD_DIM),
            held(rows, HEAD_DIM),
            held(rows, HEAD_DIM),
            held(*square),
            held(*square),
            pltpu.VMEM((ctx_count,) + square, BF16),
            pltpu.VMEM((ctx_count,) + square, F32),
            pltpu.VMEM((ctx_count,) + square, F32),
            pltpu.VMEM((ctx_count,) + square, F32),
            pltpu.VMEM((ctx_count,) + square, F32),
            pltpu.SemaphoreType.DMA,
        ]
        + [
            pltpu.SemaphoreType.DMA((count,))
            for count in (head_count,) * 3 + (heads, ctx_count) * 3 + (ctx_count, heads) * 2
        ],
        compiler_params=pltpu.CompilerParams(
            collective_id=0, has_side_effects=True, vmem_limit_bytes=56 * 1024 * 1024
        ),
    )(
        queries,
        key_input,
        value_input,
        beta_rates.reshape(heads * house, tokens),
        out_grad,
        out_weight,
    )
    return results[:3] + (results[3].reshape(beta_rates.shape),)


def solution(mesh):
    placed = (
        P("ctx", "head"),
        P(None, "ctx", "head"),
        P(None, "ctx", "head"),
        P("head", None, "ctx"),
        P(("ctx", "head"), None),
        P("head", None),
    )
    return jax.shard_map(
        shards,
        mesh=mesh,
        in_specs=placed,
        out_specs=placed[:4],
        check_vma=False,
    )
```

time: 102 us -> 95.3 us (0.934)
  the two profiles are of different devices: /device:TPU:0 before, /device:TPU:15 now
where the time goes in v2:
time: 95.3 us; the launch traced here: 95 us
  Pallas kernels  87.6 us (92%)
  local copies, waits for them, and re-layouts  6.7 us (7%)
    pallas_call x1, Pallas kernels, shards(): pl.pallas_call(functools.partial(kernel, ctx_count, head_count), out_shap...  87.6 us
    unnamed x4, local copies, waits for them, and re-layouts  6.7 us

profile of v2, /device:TPU:15, one launch (start us, length us, event | category | flops | bytes accessed | tf_op | source)
XLA Modules:
  0.0 95.0 jit_solution(4174739389098531466)
XLA Ops:
  0.6 87.6 %shard_map.93 = (bf16[128,1024]{1,0:T(8,128)(2,1)}, bf16[2,128,1024]{2,1,0:T(8,128)(2,1)}, bf16[2,128,1024]{2,1,0:T(8,128)(2,1)}, f32[16,128]{1,0:T(8,128)}) custom-call(bf16[128,1024]{1,0:T(8,128)(2,1)} %query_ref.1, bf16[2,128,1024]{2,1,0:T(8,128)(2,1)} %raw_ref.1, bf16[2,128,1024]{2,1,0:T(8,128)(2,1)} %value_ref.1, f32[16,128]{1,0:T(8,128)} %bitcast.3, ...), custom_call_target="tpu_custom_call" | custom-call | tf_op jit(solution)/shard_map/pallas_call | solution.py:408
  88.3 1.7 %copy.14 = bf16[128,1024]{1,0:T(8,128)(2,1)} copy(bf16[128,1024]{1,0:T(8,128)(2,1)} %get-tuple-element.16) | data formatting | bytes 524288
  89.9 1.9 %copy.15 = bf16[2,128,1024]{2,1,0:T(8,128)(2,1)} copy(bf16[2,128,1024]{2,1,0:T(8,128)(2,1)} %get-tuple-element.17) | data formatting | bytes 1048576
  91.8 1.9 %copy.16 = bf16[2,128,1024]{2,1,0:T(8,128)(2,1)} copy(bf16[2,128,1024]{2,1,0:T(8,128)(2,1)} %get-tuple-element.18) | data formatting | bytes 1048576
  93.7 1.3 %copy.17 = f32[8,2,128]{2,1,0:T(2,128)} copy(f32[8,2,128]{2,1,0:T(2,128)} %bitcast.2) | data formatting | bytes 16384

commit v3 on v2

--- a/solution.py
+++ b/solution.py
@@ -13,8 +13,8 @@
 BF16 = jnp.bfloat16
 SOLVER = BF16
 SPLIT = {
-    "gram": "lr", "inv1": "lr", "inv2": "lr", "sk": "lr", "sv": "lr", "dec": "lr", "off": "lr", "sc": "lr", "rd": "lr", "w": "lr",
-    "gw1": "lr", "gs": "lr", "q2": "lr", "k1": "lr", "gw2": "lr", "un": "lr", "gg": "lr", "k2": "lr", "k4": "lr",
+    "inv": "lr", "sk": "l", "sv": "l", "maps": "r", "rd": "lr", "w": "", "gs": "", "q1": "",
+    "q2": "", "k1": "", "gw2": "", "un": "r", "gg": "", "k2": "", "k4": "l",
 }
 
 
@@ -40,25 +40,39 @@
 
 def inverse(strict_system, tokens, house):
     shape = strict_system.shape
-    row, column = order(shape, 0, tokens, house), order(shape, 1, tokens, house)
-    result = jnp.where(row == column, 1.0, 0.0).astype(F32)
-    size = 1
-    while size < shape[0]:
-        joins = (row // (2 * size) == column // (2 * size)) & (row // size != column // size)
-        corner = jnp.where(joins, strict_system, 0.0)
-        if size == 1:
-            result = result - corner
+    rows = shape[0]
+    apart = order(shape, 0, tokens, house) ^ order(shape, 1, tokens, house)
+    result = -jnp.where(apart == 1, strict_system, 0.0)
+    size = 2
+    while size < rows:
+        corner = jnp.where((apart >= size) & (apart < 2 * size), strict_system, 0.0)
+        span = size // house
+        if span % 8:
+            half = corner + product(corner, result, 1, 0, SPLIT["inv"])
+            result = result - half - product(result, half, 1, 0, SPLIT["inv"])
         else:
-            half = product(corner, result, 1, 0, SPLIT["inv1"])
-            result = result - product(result, half, 1, 0, SPLIT["inv2"])
+            pairs = (house, tokens // (2 * span), 2, span, rows)
+
+            def second(array):
+                return array.reshape(pairs)[:, :, 1].reshape(rows // 2, rows)
+
+            def joined(first, last):
+                parts = [part.reshape(pairs[:2] + (1, span, rows)) for part in (first, last)]
+                return jnp.concatenate(parts, axis=2).reshape(shape)
+
+            half = second(corner)
+            half = half + product(half, result, 1, 0, SPLIT["inv"])
+            lower = second(result)
+            whole = joined(jnp.zeros_like(half), half)
+            lower = lower - half - product(lower, whole, 1, 0, SPLIT["inv"])
+            result = joined(result.reshape(pairs)[:, :, 0].reshape(rows // 2, rows), lower)
         size *= 2
     return result
 
 
-def normalize(raw):
+def scaling_of(raw):
     raw = raw.astype(F32)
-    scaling = lax.rsqrt(jnp.sum(raw * raw, axis=-1, keepdims=True) + 1e-06)
-    return raw * scaling, scaling
+    return lax.rsqrt(jnp.sum(raw * raw, axis=-1, keepdims=True) + 1e-06)
 
 
 def read_mask(tokens, rows):
@@ -71,51 +85,59 @@
     return order(shape, 1, tokens, house) < order(shape, 0, tokens, house)
 
 
-def solve_part(query, raw, value, rate, house):
+def solve_part(query, raw, value, rate, rate_row, house):
     tokens = query.shape[0]
-    query = query.astype(F32) * HEAD_DIM ** (-0.5)
-    key, _ = normalize(raw)
-    gram = product(key, key, 1, 1, SPLIT["gram"])
-    gram = jnp.where(strict_mask(tokens, house), gram, 0.0)
+    rows = raw.shape[0]
+    scaling = scaling_of(raw)
+    index = [lax.broadcasted_iota(jnp.int32, (rows, rows), axis) for axis in (0, 1)]
+    scaling_row = jnp.sum(jnp.where(index[0] == index[1], scaling, 0.0), axis=0, keepdims=True)
+    gram = product(raw, raw, 1, 1)
+    gram = jnp.where(strict_mask(tokens, house), gram * scaling * scaling_row, 0.0)
     solver = inverse(gram * rate, tokens, house)
-    solved_k = product(solver, key * rate, 1, 0, SPLIT["sk"])
-    solved_v = product(solver, value.astype(F32) * rate, 1, 0, SPLIT["sv"])
-    decay = product(key, solved_k, 0, 0, SPLIT["dec"])
-    offset = product(key, solved_v, 0, 0, SPLIT["off"])
-    scores = jnp.where(read_mask(tokens, gram.shape[0]), product(query, key, 1, 1, SPLIT["sc"]), 0.0)
-    reading = query - product(scores, solved_k, 1, 0, SPLIT["rd"])
-    return gram, solver, solved_k, solved_v, decay, offset, scores, reading
-
-
-def early_part(query, raw, value, gram, solved_k, solved_v, scores, grad, state):
+    scaled_raw = raw.astype(F32) * (scaling * rate)
+    solved_k = scaled_raw + product(solver * (rate_row * scaling_row), raw, 1, 0, SPLIT["sk"])
+    solved_v = value.astype(F32) * rate + product(solver * rate_row, value, 1, 0, SPLIT["sv"])
+    both = jnp.concatenate([solved_k * scaling, solved_v * scaling], axis=1)
+    maps = product(raw, both, 0, 0, SPLIT["maps"])
+    scores = product(query, raw, 1, 1) * (scaling_row * HEAD_DIM ** (-0.5))
+    scores = jnp.where(read_mask(tokens, rows), scores, 0.0)
+    reading = query.astype(F32) * HEAD_DIM ** (-0.5) - product(scores, solved_k, 1, 0, SPLIT["rd"])
+    return (
+        gram, solver, solved_k, solved_v, maps[:, :HEAD_DIM], maps[:, HEAD_DIM:], scores, reading,
+        jnp.broadcast_to(scaling_row, (8, rows)),
+    )
+
+
+def early_part(query, raw, value, gram, solved_k, solved_v, scores, scaling_row, grad, state):
     tokens = query.shape[0]
-    query = query.astype(F32) * HEAD_DIM ** (-0.5)
-    key, _ = normalize(raw)
     weighted = product(solved_k, state, 1, 0, SPLIT["w"]) - solved_v
-    errors = product(key, state, 1, 0) - value.astype(F32) - product(gram, weighted, 1, 0)
-    grad_weighted = -product(scores, grad, 0, 0, SPLIT["gw1"])
-    grad_scores = product(grad, weighted, 1, 1, SPLIT["gs"])
-    grad_scores = jnp.where(read_mask(tokens, raw.shape[0]), -grad_scores, 0.0)
-    grad_query = product(grad, state, 1, 1, "r") + product(grad_scores, key, 1, 0, SPLIT["q2"])
+    errors = product(raw, state, 1, 0) * scaling_of(raw) - value.astype(F32)
+    errors = errors - product(gram, weighted, 1, 0)
+    grad_weighted = -product(scores, grad, 0, 0)
+    grad_scores = -product(grad, weighted, 1, 1, SPLIT["gs"]) * HEAD_DIM ** (-0.5)
+    grad_scores = jnp.where(read_mask(tokens, raw.shape[0]), grad_scores, 0.0)
+    grad_query = product(grad, state, 1, 1, SPLIT["q1"]) * HEAD_DIM ** (-0.5)
+    grad_query = grad_query + product(grad_scores * scaling_row, raw, 1, 0, SPLIT["q2"])
     grad_key = product(grad_scores, query, 0, 0, SPLIT["k1"])
-    return weighted, errors, grad_weighted, grad_query * HEAD_DIM ** (-0.5), grad_key
-
-
-def late_part(raw, rate, solver, weighted, errors, grad_weighted, grad_key, state, adjoint, house):
+    return weighted, errors, grad_weighted, grad_query, grad_key
+
+
+def late_part(
+    raw, rate, solver, scaling_row, weighted, errors, grad_weighted, grad_key, state, adjoint, house
+):
     tokens = raw.shape[0] // house
-    key, scaling = normalize(raw)
-    grad_weighted = grad_weighted - product(key, adjoint, 1, 0, SPLIT["gw2"])
-    unscaled = product(solver, grad_weighted, 0, 0, SPLIT["un"])
+    scaling = scaling_of(raw)
+    key = raw.astype(F32) * scaling
+    grad_weighted = grad_weighted - product(raw, adjoint, 1, 0, SPLIT["gw2"]) * scaling
+    unscaled = grad_weighted + product(solver, grad_weighted, 0, 0, SPLIT["un"])
     pulled = unscaled * rate
     grad_rate = jnp.sum(errors * unscaled, axis=1, keepdims=True)
-    grad_gram = -jnp.where(strict_mask(tokens, house), product(pulled, weighted, 1, 1, SPLIT["gg"]), 0.0)
-    grad_key = (
-        grad_key
-        - product(weighted, adjoint, 1, 1, SPLIT["k2"])
-        + product(pulled, state, 1, 1, SPLIT["k2"])
-        + product(grad_gram, key, 1, 0, SPLIT["k4"])
-        + product(grad_gram, key, 0, 0, SPLIT["k4"])
-    )
+    grad_gram = jnp.where(strict_mask(tokens, house), product(pulled, weighted, 1, 1, SPLIT["gg"]), 0.0)
+    grad_gram = (grad_gram + jnp.transpose(grad_gram)) * scaling_row
+    rows_side = jnp.concatenate([-weighted, pulled], axis=1)
+    state_side = jnp.concatenate([adjoint, state], axis=1)
+    grad_key = grad_key + product(rows_side, state_side, 1, 1, SPLIT["k2"])
+    grad_key = grad_key - product(grad_gram, raw, 1, 0, SPLIT["k4"])
     along = jnp.sum(grad_key * key, axis=1, keepdims=True)
     grad_raw = scaling * (grad_key - key * along)
     return grad_raw, -pulled, grad_rate
@@ -128,7 +150,7 @@
     out_query, out_key, out_value, out_rate,
     weight, gathered, rates, grads,
     gram, solver, solved_k, solved_v, decay, offset, scores, reading, local_grad,
-    errors, grad_weighted, grad_key, state, adjoint,
+    scalings, errors, grad_weighted, grad_key, state, adjoint,
     decay_in, offset_in, grad_in, states, adjoints,
     weight_sem, up_send, down_send, gather_recv,
     decay_send, decay_recv, offset_send, offset_recv, grad_send, grad_recv,
@@ -245,9 +267,10 @@
 
     def solve_head(head):
         results = solve_part(
-            query_ref[:, columns(head)], load(raw_ref, head), load(value_ref, head), rate_of(head), house
+            query_ref[:, columns(head)], load(raw_ref, head), load(value_ref, head), rate_of(head),
+            jnp.concatenate([rate_ref[pl.ds(head * house + j, 1)] for j in range(house)], axis=1), house,
         )
-        kept = (gram, solver, solved_k, solved_v, decay, offset, scores, reading)
+        kept = (gram, solver, solved_k, solved_v, decay, offset, scores, reading, scalings)
         for ref, result in zip(kept, results):
             ref[head] = result.astype(ref.dtype)
 
@@ -331,7 +354,7 @@
             head = turn * together + part
             results = early_part(
                 query_ref[:, columns(head)], load(raw_ref, head), load(value_ref, head), gram[head],
-                solved_k[head], solved_v[head], scores[head], grads[head], state[head],
+                solved_k[head], solved_v[head], scores[head], scalings[head, 0:1], grads[head], state[head],
             )
             solved_v[head], errors[head], grad_weighted[head] = results[:3]
             out_query[:, columns(head)] = results[3].astype(BF16)
@@ -351,8 +374,8 @@
         for part in range(together):
             head = turn * together + part
             grad_raw, grad_value, grad_rate = late_part(
-                load(raw_ref, head), rate_of(head), solver[head], solved_v[head], errors[head],
-                grad_weighted[head], grad_key[head], state[head], adjoint[head], house,
+                load(raw_ref, head), rate_of(head), solver[head], scalings[head, 0:1], solved_v[head],
+                errors[head], grad_weighted[head], grad_key[head], state[head], adjoint[head], house,
             )
             out_key[:, :, columns(head)] = grad_raw.reshape(house, tokens, HEAD_DIM).astype(BF16)
             out_value[:, :, columns(head)] = grad_value.reshape(house, tokens, HEAD_DIM).astype(BF16)
@@ -392,6 +415,15 @@
         @pl.when((owner >= column) & (column > 0))
         def _():
             passing(owner, False).wait_send()
+
+
+def hand_over(*refs):
+    done = refs[-1]
+    copies = [pltpu.make_async_copy(refs[i], refs[4 + i], done.at[i]) for i in range(4)]
+    for copy in copies:
+        copy.start()
+    for copy in copies:
+        copy.wait()
 
 
 def shards(queries, key_input, value_input, beta_rates, out_grad, out_weight):
@@ -429,6 +461,7 @@
             held(tokens, rows, dtype=BF16),
             held(tokens, HEAD_DIM, dtype=BF16),
             held(*square),
+            held(8, rows),
             held(rows, HEAD_DIM),
             held(rows, HEAD_DIM),
             held(rows, HEAD_DIM),
@@ -456,7 +489,14 @@
         out_grad,
         out_weight,
     )
-    return results[:3] + (results[3].reshape(beta_rates.shape),)
+    results = pl.pallas_call(
+        hand_over,
+        out_shape=[jax.ShapeDtypeStruct(result.shape, result.dtype) for result in results],
+        in_specs=[pl.BlockSpec(memory_space=pl.ANY)] * 4,
+        out_specs=[pl.BlockSpec(memory_space=pl.ANY)] * 4,
+        scratch_shapes=[pltpu.SemaphoreType.DMA((4,))],
+    )(*results)
+    return tuple(results[:3]) + (results[3].reshape(beta_rates.shape),)
 
 
 def solution(mesh):

time: 95.3 us -> 115 us (1.21)
  Pallas kernels: 87.6 us -> 114 us
  local copies, waits for them, and re-layouts: 6.7 us -> 0 us
    pallas_call x0 -> x1, Pallas kernels: none -> 41.1 us  [shards(): pl.pallas_call(hand_over, out_shape=[jax.ShapeDtypeStruct(result.shape, r...]
    pallas_call x1, Pallas kernels: 87.6 us -> 73.2 us  [shards(): pl.pallas_call(functools.partial(kernel, ctx_count, head_count), out_shap...]
    unnamed x4 -> x0, local copies, waits for them, and re-layouts: 6.7 us -> none
where the time goes in v3:
time: 115 us
  Pallas kernels  114 us (99%)
    pallas_call x1, Pallas kernels, shards(): pl.pallas_call(functools.partial(kernel, ctx_count, head_count), out_shap...  73.2 us
    pallas_call x1, Pallas kernels, shards(): pl.pallas_call(hand_over, out_shape=[jax.ShapeDtypeStruct(result.shape, r...  41.1 us

profile of v3, /device:TPU:15, one launch (start us, length us, event | category | flops | bytes accessed | tf_op | source)
XLA Modules:
  0.0 114.9 jit_solution(10167103672074610908)
XLA Ops:
  0.6 73.2 %shard_map.93 = (bf16[128,1024]{1,0:T(8,128)(2,1)}, bf16[2,128,1024]{2,1,0:T(8,128)(2,1)}, bf16[2,128,1024]{2,1,0:T(8,128)(2,1)}, f32[16,128]{1,0:T(8,128)}) custom-call(bf16[128,1024]{1,0:T(8,128)(2,1)} %query_ref.1, bf16[2,128,1024]{2,1,0:T(8,128)(2,1)} %raw_ref.1, bf16[2,128,1024]{2,1,0:T(8,128)(2,1)} %value_ref.1, f32[16,128]{1,0:T(8,128)} %bitcast.2, ...), custom_call_target="tpu_custom_call" | custom-call | tf_op jit(solution)/shard_map/pallas_call | solution.py:440
  73.8 41.1 %shard_map.94 = (bf16[128,1024]{1,0:T(8,128)(2,1)}, bf16[2,128,1024]{2,1,0:T(8,128)(2,1)}, bf16[2,128,1024]{2,1,0:T(8,128)(2,1)}, f32[16,128]{1,0:T(8,128)}) custom-call(bf16[128,1024]{1,0:T(8,128)(2,1)} %get-tuple-element.12.refs_0_, bf16[2,128,1024]{2,1,0:T(8,128)(2,1)} %get-tuple-element.13.refs_1_, bf16[2,128,1024]{2,1,0:T(8,128)(2,1)} %get-tuple-element.14.refs_2_, ...), custom_call_target="tpu_custom_call" | custom-call | tf_op jit(solution)/shard_map/pallas_call | solution.py:492

commit v4 on v3

--- a/solution.py
+++ b/solution.py
@@ -47,9 +47,10 @@
     while size < rows:
         corner = jnp.where((apart >= size) & (apart < 2 * size), strict_system, 0.0)
         span = size // house
+        split = SPLIT["inv"] if 4 * size >= rows else ""
         if span % 8:
-            half = corner + product(corner, result, 1, 0, SPLIT["inv"])
-            result = result - half - product(result, half, 1, 0, SPLIT["inv"])
+            half = corner + product(corner, result, 1, 0, split)
+            result = result - half - product(result, half, 1, 0, split)
         else:
             pairs = (house, tokens // (2 * span), 2, span, rows)
 
@@ -61,10 +62,10 @@
                 return jnp.concatenate(parts, axis=2).reshape(shape)
 
             half = second(corner)
-            half = half + product(half, result, 1, 0, SPLIT["inv"])
+            half = half + product(half, result, 1, 0, split)
             lower = second(result)
             whole = joined(jnp.zeros_like(half), half)
-            lower = lower - half - product(lower, whole, 1, 0, SPLIT["inv"])
+            lower = lower - half - product(lower, whole, 1, 0, split)
             result = joined(result.reshape(pairs)[:, :, 0].reshape(rows // 2, rows), lower)
         size *= 2
     return result
@@ -418,12 +419,8 @@
 
 
 def hand_over(*refs):
-    done = refs[-1]
-    copies = [pltpu.make_async_copy(refs[i], refs[4 + i], done.at[i]) for i in range(4)]
-    for copy in copies:
-        copy.start()
-    for copy in copies:
-        copy.wait()
+    for source, target in zip(refs[:4], refs[4:]):
+        target[...] = source[...]
 
 
 def shards(queries, key_input, value_input, beta_rates, out_grad, out_weight):
@@ -492,9 +489,8 @@
     results = pl.pallas_call(
         hand_over,
         out_shape=[jax.ShapeDtypeStruct(result.shape, result.dtype) for result in results],
-        in_specs=[pl.BlockSpec(memory_space=pl.ANY)] * 4,
-        out_specs=[pl.BlockSpec(memory_space=pl.ANY)] * 4,
-        scratch_shapes=[pltpu.SemaphoreType.DMA((4,))],
+        in_specs=[vmem] * 4,
+        out_specs=[vmem] * 4,
     )(*results)
     return tuple(results[:3]) + (results[3].reshape(beta_rates.shape),)
 

time: 115 us -> 70.1 us (0.61)
  Pallas kernels: 114 us -> 69.3 us
    pallas_call x1, Pallas kernels: 41.1 us -> 2.37 us  [shards(): pl.pallas_call(hand_over, out_shape=[jax.ShapeDtypeStruct(result.shape, r...]
    pallas_call x1, Pallas kernels: 73.2 us -> 66.9 us  [shards(): pl.pallas_call(functools.partial(kernel, ctx_count, head_count), out_shap...]
where the time goes in v4:
time: 70.1 us; the launch traced here: 69.9 us
  Pallas kernels  69.3 us (99%)
    pallas_call x1, Pallas kernels, shards(): pl.pallas_call(functools.partial(kernel, ctx_count, head_count), out_shap...  66.9 us
    pallas_call x1, Pallas kernels, shards(): pl.pallas_call(hand_over, out_shape=[jax.ShapeDtypeStruct(result.shape, r...  2.37 us

profile of v4, /device:TPU:15, one launch (start us, length us, event | category | flops | bytes accessed | tf_op | source)
XLA Modules:
  0.0 69.9 jit_solution(3620992159129038280)
XLA Ops:
  0.6 66.9 %shard_map.93 = (bf16[128,1024]{1,0:T(8,128)(2,1)}, bf16[2,128,1024]{2,1,0:T(8,128)(2,1)}, bf16[2,128,1024]{2,1,0:T(8,128)(2,1)}, f32[16,128]{1,0:T(8,128)}) custom-call(bf16[128,1024]{1,0:T(8,128)(2,1)} %query_ref.1, bf16[2,128,1024]{2,1,0:T(8,128)(2,1)} %raw_ref.1, bf16[2,128,1024]{2,1,0:T(8,128)(2,1)} %value_ref.1, f32[16,128]{1,0:T(8,128)} %bitcast.2, ...), custom_call_target="tpu_custom_call" | custom-call | tf_op jit(solution)/shard_map/pallas_call | solution.py:437
  67.6 2.4 %shard_map.94 = (bf16[128,1024]{1,0:T(8,128)(2,1)}, bf16[2,128,1024]{2,1,0:T(8,128)(2,1)}, bf16[2,128,1024]{2,1,0:T(8,128)(2,1)}, f32[16,128]{1,0:T(8,128)}) custom-call(bf16[128,1024]{1,0:T(8,128)(2,1)} %get-tuple-element.12.refs_0_, bf16[2,128,1024]{2,1,0:T(8,128)(2,1)} %get-tuple-element.13.refs_1_, bf16[2,128,1024]{2,1,0:T(8,128)(2,1)} %get-tuple-element.14.refs_2_, ...), custom_call_target="tpu_custom_call" | custom-call | tf_op jit(solution)/shard_map/pallas_call | solution.py:489

commit v5 on v4

--- a/solution.py
+++ b/solution.py
@@ -311,7 +311,7 @@
             head = turn * together + index
             grad = block[:, index * HEAD_DIM : (index + 1) * HEAD_DIM]
             grads[head] = grad
-            local_grad[head] = product(reading[head], grad, 0, 0)
+            local_grad[head] = product(reading[head], grad, 0, 0).astype(BF16)
             give(*grad_args, head)
         return carry
 
@@ -325,7 +325,7 @@
                 to_owner(*args, mine, source).wait_recv()
 
         def forward(user, held):
-            states[user] = held
+            states[user] = held.astype(BF16)
             hand_out(*state_args, user)
             arrive(decay_args, user)
             arrive(offset_args, user)
@@ -336,7 +336,7 @@
 
         def backward(step, held):
             user = ctx_count - 1 - step
-            adjoints[user] = held
+            adjoints[user] = held.astype(BF16)
             hand_out(*adjoint_args, user)
             arrive(grad_args, user)
             return held + grad_in[user] - product(decay_in[user], held, 0, 0)
@@ -457,18 +457,18 @@
             held(*square),
             held(tokens, rows, dtype=BF16),
             held(tokens, HEAD_DIM, dtype=BF16),
-            held(*square),
+            held(*square, dtype=BF16),
             held(8, rows),
             held(rows, HEAD_DIM),
             held(rows, HEAD_DIM),
             held(rows, HEAD_DIM),
-            held(*square),
-            held(*square),
+            held(*square, dtype=BF16),
+            held(*square, dtype=BF16),
             pltpu.VMEM((ctx_count,) + square, BF16),
             pltpu.VMEM((ctx_count,) + square, F32),
-            pltpu.VMEM((ctx_count,) + square, F32),
-            pltpu.VMEM((ctx_count,) + square, F32),
-            pltpu.VMEM((ctx_count,) + square, F32),
+            pltpu.VMEM((ctx_count,) + square, BF16),
+            pltpu.VMEM((ctx_count,) + square, BF16),
+            pltpu.VMEM((ctx_count,) + square, BF16),
             pltpu.SemaphoreType.DMA,
         ]
         + [

time: 70.1 us -> 63.5 us (0.906)
  Pallas kernels: 69.3 us -> 62.7 us
    pallas_call x1, Pallas kernels: 66.9 us -> 60.3 us  [shards(): pl.pallas_call(functools.partial(kernel, ctx_count, head_count), out_shap...]
where the time goes in v5:
time: 63.5 us; the launch traced here: 63.3 us
  Pallas kernels  62.7 us (99%)
  between operations  0.64 us (1%)
    pallas_call x1, Pallas kernels, shards(): pl.pallas_call(functools.partial(kernel, ctx_count, head_count), out_shap...  60.3 us
    pallas_call x1, Pallas kernels, shards(): pl.pallas_call(hand_over, out_shape=[jax.ShapeDtypeStruct(result.shape, r...  2.37 us

profile of v5, /device:TPU:15, one launch (start us, length us, event | category | flops | bytes accessed | tf_op | source)
XLA Modules:
  0.0 63.3 jit_solution(9266653992317072309)
XLA Ops:
  0.6 60.3 %shard_map.93 = (bf16[128,1024]{1,0:T(8,128)(2,1)}, bf16[2,128,1024]{2,1,0:T(8,128)(2,1)}, bf16[2,128,1024]{2,1,0:T(8,128)(2,1)}, f32[16,128]{1,0:T(8,128)}) custom-call(bf16[128,1024]{1,0:T(8,128)(2,1)} %query_ref.1, bf16[2,128,1024]{2,1,0:T(8,128)(2,1)} %raw_ref.1, bf16[2,128,1024]{2,1,0:T(8,128)(2,1)} %value_ref.1, f32[16,128]{1,0:T(8,128)} %bitcast.2, ...), custom_call_target="tpu_custom_call" | custom-call | tf_op jit(solution)/shard_map/pallas_call | solution.py:437
  60.9 2.4 %shard_map.94 = (bf16[128,1024]{1,0:T(8,128)(2,1)}, bf16[2,128,1024]{2,1,0:T(8,128)(2,1)}, bf16[2,128,1024]{2,1,0:T(8,128)(2,1)}, f32[16,128]{1,0:T(8,128)}) custom-call(bf16[128,1024]{1,0:T(8,128)(2,1)} %get-tuple-element.12.refs_0_, bf16[2,128,1024]{2,1,0:T(8,128)(2,1)} %get-tuple-element.13.refs_1_, bf16[2,128,1024]{2,1,0:T(8,128)(2,1)} %get-tuple-element.14.refs_2_, ...), custom_call_target="tpu_custom_call" | custom-call | tf_op jit(solution)/shard_map/pallas_call | solution.py:489

commit v6 on v5

--- a/solution.py
+++ b/solution.py
@@ -454,7 +454,7 @@
             held(rows, HEAD_DIM),
             held(rows, HEAD_DIM),
             held(*square, dtype=BF16),
-            held(*square),
+            held(*square, dtype=BF16),
             held(tokens, rows, dtype=BF16),
             held(tokens, HEAD_DIM, dtype=BF16),
             held(*square, dtype=BF16),
@@ -465,7 +465,7 @@
             held(*square, dtype=BF16),
             held(*square, dtype=BF16),
             pltpu.VMEM((ctx_count,) + square, BF16),
-            pltpu.VMEM((ctx_count,) + square, F32),
+            pltpu.VMEM((ctx_count,) + square, BF16),
             pltpu.VMEM((ctx_count,) + square, BF16),
             pltpu.VMEM((ctx_count,) + square, BF16),
             pltpu.VMEM((ctx_count,) + square, BF16),

time: 63.5 us -> 59.8 us (0.942)
  Pallas kernels: 62.7 us -> 59 us
    pallas_call x1, Pallas kernels: 60.3 us -> 56.6 us  [shards(): pl.pallas_call(functools.partial(kernel, ctx_count, head_count), out_shap...]
where the time goes in v6:
time: 59.8 us; the launch traced here: 59.7 us
  Pallas kernels  59 us (99%)
  between operations  0.64 us (1%)
    pallas_call x1, Pallas kernels, shards(): pl.pallas_call(functools.partial(kernel, ctx_count, head_count), out_shap...  56.6 us
    pallas_call x1, Pallas kernels, shards(): pl.pallas_call(hand_over, out_shape=[jax.ShapeDtypeStruct(result.shape, r...  2.37 us

profile of v6, /device:TPU:15, one launch (start us, length us, event | category | flops | bytes accessed | tf_op | source)
XLA Modules:
  0.0 59.7 jit_solution(4031247804576805958)
XLA Ops:
  0.6 56.6 %shard_map.93 = (bf16[128,1024]{1,0:T(8,128)(2,1)}, bf16[2,128,1024]{2,1,0:T(8,128)(2,1)}, bf16[2,128,1024]{2,1,0:T(8,128)(2,1)}, f32[16,128]{1,0:T(8,128)}) custom-call(bf16[128,1024]{1,0:T(8,128)(2,1)} %query_ref.1, bf16[2,128,1024]{2,1,0:T(8,128)(2,1)} %raw_ref.1, bf16[2,128,1024]{2,1,0:T(8,128)(2,1)} %value_ref.1, f32[16,128]{1,0:T(8,128)} %bitcast.2, ...), custom_call_target="tpu_custom_call" | custom-call | tf_op jit(solution)/shard_map/pallas_call | solution.py:437
  57.3 2.4 %shard_map.94 = (bf16[128,1024]{1,0:T(8,128)(2,1)}, bf16[2,128,1024]{2,1,0:T(8,128)(2,1)}, bf16[2,128,1024]{2,1,0:T(8,128)(2,1)}, f32[16,128]{1,0:T(8,128)}) custom-call(bf16[128,1024]{1,0:T(8,128)(2,1)} %get-tuple-element.12.refs_0_, bf16[2,128,1024]{2,1,0:T(8,128)(2,1)} %get-tuple-element.13.refs_1_, bf16[2,128,1024]{2,1,0:T(8,128)(2,1)} %get-tuple-element.14.refs_2_, ...), custom_call_target="tpu_custom_call" | custom-call | tf_op jit(solution)/shard_map/pallas_call | solution.py:489
